TPU v7x, 512 devices: a whole 4x8x8 slice. The times are simulated.
512 devices in a mesh: dp: 32 (over y_lo, z), tensor: 16 (over y_hi, x, core).
Axes of the slice: x: 4, y: 8 (y_hi: 2, y_lo: 4; y = y_hi * 4 + y_lo), z: 8, core: 2. Of those that a mesh axis runs over, the one named last changes fastest.
Arguments:
- features: bfloat16 [65536, 4096], P(('dp', 'tensor')), may hold values from -6 to 6
- step_raw: bfloat16 [65536, 128], P(('dp', 'tensor')), may hold values from -3 to 10
- input_map: bfloat16 [65536, 8, 128], P(('dp', 'tensor')), may hold values from -0.75 to 0.75
- output_map: bfloat16 [65536, 8, 128], P(('dp', 'tensor')), may hold values from -0.75 to 0.75
- decay_log: float32 [128], P('tensor'), may hold values from -10 to -2
- skip_gain: float32 [128], P('tensor'), may hold values from 0.1 to 1.9
- saved_states: bfloat16 [32, 7, 128, 32, 128], P('dp', None, 'tensor'), may hold values from -6 to 6
- grad_out: bfloat16 [65536, 4096], P(('dp', 'tensor')), may hold values from -6 to 6
Outputs:
- grad_features: bfloat16 [65536, 4096], P(('dp', 'tensor'))
- grad_step: float32 [65536, 128], P(('dp', 'tensor'))
- grad_input_map: bfloat16 [65536, 8, 128], P(('dp', 'tensor'))
- grad_output_map: bfloat16 [65536, 8, 128], P(('dp', 'tensor'))
- grad_decay_log: float32 [128], P('tensor')
- grad_skip_gain: float32 [128], P('tensor')
All inputs are finite; a program needn't handle non-finite values.
Results may differ from a plain program's by a relative error of at most 0.0013.
Values may be sent and summed in bfloat16 or wider, within the bound.
A program may use at most 128 MiB of HBM per device.

v0:
```python
import jax
import jax.numpy as jnp
from jax import lax
from jax.sharding import PartitionSpec as P

Q = 128


def head_forward(head_feat, head_raw, head_decay, head_skip, head_in, head_out, head_states):
    block = Q
    stretches = head_feat.shape[0] // block
    pairs = stretches // 2
    exact = lax.Precision.HIGHEST
    step = jax.nn.softplus(head_raw)
    rate = -jnp.exp(head_decay) * step
    cum = jnp.cumsum(rate.reshape(stretches, block), axis=1)
    feat_c = head_feat.reshape(stretches, block, -1)
    in_c = head_in.reshape(stretches, block, -1)
    out_c = head_out.reshape(stretches, block, -1)
    step_c = step.reshape(stretches, block)
    inside = jnp.arange(block)[:, None] >= jnp.arange(block)[None, :]
    spread = cum[:, :, None] - cum[:, None, :]
    decay = jnp.where(inside, jnp.exp(jnp.where(inside, spread, 0.0)), 0.0)
    scores = jnp.einsum("cin,cjn->cij", out_c, in_c, precision=exact) * decay * step_c[:, None, :]
    within = jnp.einsum("cij,cjp->cip", scores, feat_c, precision=exact)
    weight_end = jnp.exp(cum[:, -1:] - cum) * step_c
    added = jnp.einsum("cjp,cjn->cpn", feat_c * weight_end[:, :, None], in_c, precision=exact)
    falloff = jnp.exp(cum[:, -1])
    saved_pad = jnp.concatenate([head_states, jnp.zeros_like(head_states[:1])], axis=0)
    following = jnp.stack([jnp.zeros_like(saved_pad), saved_pad], axis=1).reshape(
        stretches, head_states.shape[1], head_states.shape[2]
    )
    resets = jnp.tile(jnp.array([0.0, 1.0], jnp.float32), pairs)

    def advance(state, items):
        factor, extra, coming, reset = items
        made = factor * state + extra
        return (made + reset * (coming - lax.stop_gradient(made)), state)

    start_state = jnp.zeros((head_states.shape[1], head_states.shape[2]), jnp.float32)
    ending, entering = lax.scan(advance, start_state, (falloff, added, following, resets))
    across = jnp.einsum("cin,cpn->cip", out_c * jnp.exp(cum)[:, :, None], entering, precision=exact)
    return (within + across).reshape(head_feat.shape) + head_skip * head_feat


def head_backward(
    head_feat, head_raw, head_decay, head_skip, head_in, head_out, head_states, head_cot
):

    def forward(a_feat, a_raw, a_decay, a_skip, a_in, a_out):
        return head_forward(a_feat, a_raw, a_decay, a_skip, a_in, a_out, head_states)

    ignored, pull = jax.vjp(forward, head_feat, head_raw, head_decay, head_skip, head_in, head_out)
    return pull(head_cot)


def on_device(
    features, step_raw, input_map, output_map, decay_log, skip_gain, saved_states, grad_out
):
    tensor_size = lax.axis_size("tensor")
    tok_rows = features.shape[0]
    seq_rows = tok_rows * tensor_size
    heads_all = step_raw.shape[1]
    heads_here = heads_all // tensor_size
    groups = input_map.shape[1]
    state_width = input_map.shape[2]
    per_group = heads_all // groups
    head_width = saved_states.shape[3]
    copies = per_group // heads_here
    slot_in = jnp.repeat(input_map, copies, axis=1)
    slot_out = jnp.repeat(output_map, copies, axis=1)
    span = min(per_group, heads_here)
    feats, cotan, raws, inputs, outputs = (
        lax.all_to_all(features, "tensor", split_axis=1, concat_axis=0, tiled=True),
        lax.all_to_all(grad_out, "tensor", split_axis=1, concat_axis=0, tiled=True),
        lax.all_to_all(step_raw, "tensor", split_axis=1, concat_axis=0, tiled=True),
        lax.all_to_all(slot_in, "tensor", split_axis=1, concat_axis=0, tiled=True),
        lax.all_to_all(slot_out, "tensor", split_axis=1, concat_axis=0, tiled=True),
    )
    local_groups = inputs.shape[1]
    head_feats = jnp.transpose(feats.reshape(seq_rows, heads_here, head_width), (1, 0, 2)).astype(
        jnp.float32
    )
    head_cots = jnp.transpose(cotan.reshape(seq_rows, heads_here, head_width), (1, 0, 2)).astype(
        jnp.float32
    )
    head_raws = jnp.transpose(raws).astype(jnp.float32)
    head_ins = jnp.repeat(jnp.transpose(inputs, (1, 0, 2)), span, axis=0).astype(jnp.float32)
    head_outs = jnp.repeat(jnp.transpose(outputs, (1, 0, 2)), span, axis=0).astype(jnp.float32)
    head_states = jnp.transpose(saved_states[0], (1, 0, 2, 3)).astype(jnp.float32)
    d_feat, d_raw, grad_decay, grad_skip, d_in, d_out = jax.vmap(head_backward)(
        head_feats, head_raws, decay_log, skip_gain, head_ins, head_outs, head_states, head_cots
    )
    grad_feat = jnp.transpose(d_feat, (1, 0, 2)).reshape(seq_rows, heads_here * head_width)
    grad_raw = jnp.transpose(d_raw)
    grad_in = jnp.transpose(
        d_in.reshape(local_groups, span, seq_rows, state_width).sum(axis=1), (1, 0, 2)
    )
    grad_outmap = jnp.transpose(
        d_out.reshape(local_groups, span, seq_rows, state_width).sum(axis=1), (1, 0, 2)
    )
    total_decay, total_skip = lax.psum((grad_decay, grad_skip), "dp")
    back_feat = lax.all_to_all(
        grad_feat.astype(jnp.bfloat16), "tensor", split_axis=0, concat_axis=1, tiled=True
    )
    back_raw, back_in, back_out = (
        lax.all_to_all(grad_raw, "tensor", split_axis=0, concat_axis=1, tiled=True),
        lax.all_to_all(grad_in, "tensor", split_axis=0, concat_axis=1, tiled=True),
        lax.all_to_all(grad_outmap, "tensor", split_axis=0, concat_axis=1, tiled=True),
    )
    back_in = back_in.reshape(tok_rows, groups, copies, state_width).sum(axis=2)
    back_out = back_out.reshape(tok_rows, groups, copies, state_width).sum(axis=2)
    return (
        back_feat,
        back_raw,
        back_in.astype(jnp.bfloat16),
        back_out.astype(jnp.bfloat16),
        total_decay,
        total_skip,
    )


def solution(mesh):
    placed = (
        P(("dp", "tensor"), None),
        P(("dp", "tensor"), None),
        P(("dp", "tensor"), None, None),
        P(("dp", "tensor"), None, None),
        P("tensor"),
        P("tensor"),
        P("dp", None, "tensor", None, None),
        P(("dp", "tensor"), None),
    )
    return jax.shard_map(
        on_device,
        mesh=mesh,
        in_specs=placed,
        out_specs=(
            P(("dp", "tensor"), None),
            P(("dp", "tensor"), None),
            P(("dp", "tensor"), None, None),
            P(("dp", "tensor"), None, None),
            P("tensor"),
            P("tensor"),
        ),
        check_vma=False,
    )
```

profile of v0, /device:TPU:32, one launch (start us, length us, event | category | flops | bytes accessed | tf_op | source)
XLA Modules:
  0.0 461.5 jit_solution(10315054663098287562)
XLA Ops:
  0.6 1.6 copy.165
  2.2 9.7 %all-to-all-start.2 = ((bf16[128,16,8]{0,2,1:T(8,128)(2,1)}), bf16[128,16,8]{0,2,1:T(8,128)(2,1)S(1)}, u32[]{:S(2)}, u32[]{:S(2)}) async-start(bf16[128,16,8]{0,2,1:T(8,128)(2,1)} %bitcast.7), calls=%async_computation.2 | async-start | bytes 65536 | tf_op jit(solution)/shard_map/all_to_all | solution.py:76
  11.9 1.1 copy.164
  13.0 3.6 all-to-all-done.2
  17.5 8.8 %all-to-all-start.1 = ((bf16[128,16,128]{0,2,1:T(8,128)(2,1)}), bf16[128,16,128]{0,2,1:T(8,128)(2,1)S(1)}, u32[]{:S(2)}, u32[]{:S(2)}) async-start(bf16[128,16,128]{0,2,1:T(8,128)(2,1)} %bitcast.3), calls=%async_computation.1 | async-start | bytes 1048576 | tf_op jit(solution)/shard_map/all_to_all | solution.py:78
  26.3 2.3 copy.168
  28.6 9.0 %all-to-all-done.1 = bf16[128,16,128]{0,2,1:T(8,128)(2,1)S(1)} async-done(((bf16[128,16,128]{0,2,1:T(8,128)(2,1)}), bf16[128,16,128]{0,2,1:T(8,128)(2,1)S(1)}, u32[]{:S(2)}, u32[]{:S(2)}) %all-to-all-start.1) | async-done | bytes 524320 | tf_op jit(solution)/shard_map/all_to_all | solution.py:78
  37.6 9.0 %all-to-all-start.3 = ((bf16[128,16,256]{0,2,1:T(8,128)(2,1)}), bf16[128,16,256]{0,2,1:T(8,128)(2,1)S(1)}, u32[]{:S(2)}, u32[]{:S(2)}) async-start(bf16[128,16,256]{0,2,1:T(8,128)(2,1)} %bitcast.15), calls=%async_computation.3 | async-start | bytes 2097152 | tf_op jit(solution)/shard_map/all_to_all | solution.py:74
  46.7 1.3 copy.162
  48.0 13.9 %all-to-all-done.3 = bf16[128,16,256]{0,2,1:T(8,128)(2,1)S(1)} async-done(((bf16[128,16,256]{0,2,1:T(8,128)(2,1)}), bf16[128,16,256]{0,2,1:T(8,128)(2,1)S(1)}, u32[]{:S(2)}, u32[]{:S(2)}) %all-to-all-start.3) | async-done | bytes 1048608 | tf_op jit(solution)/shard_map/all_to_all | solution.py:74
  61.9 17.8 %all-to-all-start = ((bf16[128,16,256]{0,2,1:T(8,128)(2,1)}), bf16[128,16,256]{0,2,1:T(8,128)(2,1)S(1)}, u32[]{:S(2)}, u32[]{:S(2)}) async-start(bf16[128,16,256]{0,2,1:T(8,128)(2,1)} %bitcast.271), calls=%async_computation | async-start | bytes 2097152 | tf_op jit(solution)/shard_map/all_to_all | solution.py:75
  81.9 1.6 copy.172
  83.6 11.3 %all-to-all-done = bf16[128,16,256]{0,2,1:T(8,128)(2,1)S(1)} async-done(((bf16[128,16,256]{0,2,1:T(8,128)(2,1)}), bf16[128,16,256]{0,2,1:T(8,128)(2,1)S(1)}, u32[]{:S(2)}, u32[]{:S(2)}) %all-to-all-start) | async-done | bytes 1048608 | tf_op jit(solution)/shard_map/all_to_all | solution.py:75
  96.1 17.8 %all-to-all-start.4 = ((bf16[128,16,128]{2,0,1:T(8,128)(2,1)}), bf16[128,16,128]{2,0,1:T(8,128)(2,1)S(1)}, u32[]{:S(2)}, u32[]{:S(2)}) async-start(bf16[128,16,128]{2,0,1:T(8,128)(2,1)} %bitcast.18), calls=%async_computation.4 | async-start | bytes 1048576 | tf_op jit(solution)/shard_map/all_to_all | solution.py:77
  114.5 2.3 reduce_window_sum.22
  118.2 1.2 bitcast_convert_fusion
  119.4 1.6 copy.169
  121.0 1.5 reshape.169
  122.5 2.9 copy.163
  125.4 1.5 reshape.164
  127.0 4.7 %fusion.60 = f32[16,8,32,128]{3,2,0,1:T(8,128)} fusion(bf16[16,128,128]{2,1,0:T(8,128)(2,1)S(1)} %bitcast.262, f32[8,16,128]{2,1,0:T(8,128)S(1)} %get-tuple-element.391, bf16[2048,8,32]{0,2,1:T(8,128)(2,1)S(1)} %reshape.169), kind=kOutput, calls=%fused_computation.73 | convolution fusion | flops 806354944 | bytes 3735552 | tf_op jit(solution)/shard_map/vmap(jvp(cjp,cjn->cpn))/dot_general | solution.py:27
  131.6 48.2 %while.32 = (s32[]{:T(128)}, f32[8,32,128]{2,1,0:T(8,128)S(1)}, f32[16,8,32,128]{3,2,1,0:T(8,128)}, f32[16,8]{1,0:T(8,128)S(1)}, f32[16,8,32,128]{3,2,0,1:T(8,12...) while((s32[]{:T(128)}, f32[8,32,128]{2,1,0:T(8,128)S(1)}, ...), condition=%wide.region_2.3_spmd.clone, body=%wide.region_1.2_spmd.clone.sunk | while | flops 229379 | bytes 786668 | solution.py:41
  132.9 1.7 fusion.112
  135.9 1.7 fusion.112
  138.9 1.7 fusion.112
  141.8 1.7 fusion.112
  144.8 1.7 fusion.112
  147.8 1.7 fusion.112
  150.8 1.7 fusion.112
  153.8 1.7 fusion.112
  156.8 1.7 fusion.112
  159.7 1.7 fusion.112
  162.7 1.7 fusion.112
  165.7 1.7 fusion.112
  168.7 1.7 fusion.112
  171.7 1.7 fusion.112
  174.7 1.7 fusion.112
  177.6 1.7 fusion.112
  179.9 4.5 fusion.68
  184.4 8.0 %fusion.63 = f32[16,8,32,128]{3,2,0,1:T(8,128)} fusion(f32[8,16,128]{2,1,0:T(8,128)S(1)} %get-tuple-element.392, f32[16,128,128]{1,2,0:T(8,128)S(1)} %copy-done.3, bf16[2048,8,32]{0,2,1:T(8,128)(2,1)S(1)} %reshape.164), kind=kOutput, calls=%fused_computation.74 | convolution fusion | flops 807403520 | bytes 4259840 | tf_op jit(solution)/shard_map/vmap(transpose(jvp(cin,cpn->cip)))/dot_general | solution.py:42
  192.5 9.7 %fusion.5 = (f32[8,16,128]{2,1,0:T(8,128)}, f32[8,16,128,128]{3,2,1,0:T(8,128)}) fusion(f32[16,128,128]{1,2,0:T(8,128)S(1)} %copy-done.3, f32[16,8,32,128]{3,2,1,0:T(8,128)S(1)} %copy-done.5, bf16[2048,8,32]{0,2,1:T(8,128)(2,1)S(1)} %reshape.164), kind=kOutput, calls=%fused_computation.15 | convolution fusion | flops 809484288 | bytes 12648448 | tf_op jit(solution)/shard_map/vmap(transpose(jvp(cin,cpn->cip)))/dot_general | solution.py:42
  202.4 19.7 %while.33 = (s32[]{:T(128)}, f32[8,32,128]{2,1,0:T(8,128)S(1)}, f32[16,8]{1,0:T(8,128)S(1)}, f32[16,8,32,128]{3,2,0,1:T(8,128)S(1)}, f32[16,8,32,128]{3,2,0,1:T(...) while((s32[]{:T(128)}, f32[8,32,128]{2,1,0:T(8,128)S(1)}, ...), condition=%wide.region_5.6_spmd.clone, body=%wide.region_3.5_spmd.clone.sunk | while | flops 196604 | bytes 786772 | solution.py:41
  202.5 1.1 fusion.114
  203.7 1.1 fusion.114
  204.9 1.1 fusion.114
  206.1 1.1 fusion.114
  207.3 1.1 fusion.114
  208.6 1.1 fusion.114
  222.1 9.0 %fusion.40 = (f32[8,16,128]{2,1,0:T(8,128)S(1)}, f32[8,16,32,128]{3,2,1,0:T(8,128)}) fusion(f32[16,8,32,128]{3,2,0,1:T(8,128)S(1)} %get-tuple-element.186, bf16[16,128,128]{2,1,0:T(8,128)(2,1)} %bitcast.263, bf16[2048,8,32]{0,2,1:T(8,128)(2,1)S(1)} %reshape.169), kind=kOutput, calls=%fused_computation.56 | convolution fusion | flops 806862848 | bytes 5832704 | tf_op jit(solution)/shard_map/vmap(transpose(jvp(cjp,cjn->cpn)))/dot_general | solution.py:27
  232.9 9.7 %fusion.82 = (f32[8,16,128]{2,1,0:T(8,128)S(1)}, f32[8,16,128]{2,1,0:T(8,128)S(1)}, f32[8,16,128]{2,1,0:T(8,128)S(1)}, f32[8,16,128,128]{3,2,1,0:T(8,128)}) fusion(f32[8,16,128]{2,1,0:T(8,128)S(1)} %reduce_window_sum.22, f32[8,16,128,128]{3,2,1,0:T(8,128)} %fusion.68, f32[8,16,128]{2,1,0:T(8,128)} %get-tuple-element.400, ...), kind=kOutput, calls=%fused_computation.94 | convolution fusion | flops 564084736 | bytes 18169856 | tf_op jit(solution)/shard_map/vmap(jvp(cin,cjn->cij))/dot_general | solution.py:24
  243.4 10.6 %reduce_window_sum.23 = f32[8,16,128]{2,1,0:T(8,128)S(1)} reduce-window(f32[8,16,128]{2,1,0:T(8,128)} %get-tuple-element.387, f32[]{:T(128)} %constant.83.clone.1), window={size=1x1x128 pad=0_0x0_0x0_127}, to_apply=%region_12.13 | reduce-window | flops 2080768 | bytes 131076 | tf_op jit(solution)/shard_map/vmap(transpose(jvp(jit(cumsum))))/reduce_window_sum | solution.py:16
  254.0 1.7 fusion.88
  255.7 9.6 %all-to-all-start.6 = ((f32[16,128,8]{1,2,0:T(8,128)}), f32[16,128,8]{1,2,0:T(8,128)S(1)}, u32[]{:S(2)}, u32[]{:S(2)}) async-start(f32[16,128,8]{1,2,0:T(8,128)} %get-tuple-element.390), calls=%async_computation.6 | async-start | bytes 131072 | tf_op jit(solution)/shard_map/all_to_all | solution.py:107
  265.3 9.5 %fusion.42 = f32[8,16,4,8,128]{4,3,2,1,0:T(8,128)S(1)} fusion(f32[8,16,32,128]{3,2,1,0:T(8,128)} %get-tuple-element.397, f32[8,16,128,128]{3,2,1,0:T(8,128)} %get-tuple-element.395, f32[8,16,128]{2,1,0:T(8,128)} %get-tuple-element.400, f32[8,16,128]{2,1,0:T(8,128)S(1)} %reduce_window_sum.22, pred[128,128]{1,0:T(8,128)(4,1)S(1)} %iota_compare_fusion, ...), kind=kOutput, calls=%fused_computation.59 | convolution fusion | flops 816840704 | bytes 13844480 | tf_op jit(solution)/shard_map/vmap(transpose(jvp(cij,cjp->cip)))/dot_general | solution.py:25
  275.7 1.2 copy.181
  277.0 10.0 %all-to-all-start.5 = ((bf16[16,128,256]{1,2,0:T(8,128)(2,1)}), bf16[16,128,256]{1,2,0:T(8,128)(2,1)}, u32[]{:S(2)}, u32[]{:S(2)}) async-start(bf16[16,128,256]{1,2,0:T(8,128)(2,1)} %copy.181), calls=%async_computation.5 | async-start | bytes 2097152 | tf_op jit(solution)/shard_map/all_to_all | solution.py:103
  287.0 11.9 %fusion.18 = f32[8,16,128,128]{3,2,1,0:T(8,128)S(1)} fusion(f32[8,16,128,128]{3,2,1,0:T(8,128)} %fusion.68, f32[8,16,128]{2,1,0:T(8,128)S(1)} %copy-done.12, f32[8,16,128]{2,1,0:T(8,128)S(1)} %reduce_window_sum.22, pred[128,128]{1,0:T(8,128)(4,1)S(1)} %iota_compare_fusion, bf16[16,128,128]{2,1,0:T(8,128)(2,1)} %copy.178), kind=kOutput, calls=%fused_computation.30 | convolution fusion | flops 3231711232 | bytes 17448960 | tf_op jit(solution)/shard_map/vmap(transpose(jvp(cin,cjn->cij)))/dot_general | solution.py:24
  298.9 14.5 %add_reduce_fusion = f32[16,128,128]{2,1,0:T(8,128)} fusion(f32[8,16,128,128]{3,2,1,0:T(8,128)S(1)} %fusion.18, f32[16,8,32,128]{3,2,0,1:T(8,128)S(1)} %get-tuple-element.186, f32[8,16,128]{2,1,0:T(8,128)S(1)} %get-tuple-element.391, bf16[2048,8,32]{0,2,1:T(8,128)(2,1)S(1)} %reshape.169), kind=kOutput, calls=%fused_computation.18 | convolution fusion | flops 810287104 | bytes 12648448 | tf_op jit(solution)/shard_map/vmap(transpose(jvp(cjp,cjn->cpn)))/dot_general | solution.py:27
  313.4 10.0 %all-to-all-start.7 = ((f32[2048,1,128]{2,1,0:T(1,128)}), f32[2048,1,128]{2,1,0:T(1,128)S(1)}, u32[]{:S(2)}, u32[]{:S(2)}) async-start(f32[2048,1,128]{2,1,0:T(1,128)} %bitcast.267), calls=%async_computation.7 | async-start | bytes 2097152 | tf_op jit(solution)/shard_map/all_to_all | solution.py:108
  323.4 15.2 %fusion.7 = f32[16,128,128]{1,2,0:T(8,128)S(1)} fusion(f32[8,16,128,128]{3,2,1,0:T(8,128)} %get-tuple-element.399, f32[8,16,128]{2,1,0:T(8,128)S(1)} %copy-done.14, bf16[16,128,128]{2,1,0:T(8,128)(2,1)} %bitcast.265, f32[8,16,128,128]{3,2,1,0:T(8,128)} %fusion.68, f32[8,16,128]{2,1,0:T(8,128)S(1)} %copy-done.12, f32[8,16,128]{2,1,0:T(8,128)S(1)} %reduce_window_sum.22, ...), kind=kOutput, calls=%fused_computation.17 | convolution fusion | flops 3237740544 | bytes 18563072 | tf_op jit(solution)/shard_map/vmap(transpose(jvp(cin,cjn->cij)))/dot_general | solution.py:24
  338.6 1.3 copy.193
  340.0 16.4 %all-to-all-start.8 = ((f32[2048,1,128]{2,1,0:T(1,128)}), f32[2048,1,128]{2,1,0:T(1,128)S(1)}, u32[]{:S(2)}, u32[]{:S(2)}) async-start(f32[2048,1,128]{2,1,0:T(1,128)} %bitcast.47), calls=%async_computation.8 | async-start | bytes 2097152 | tf_op jit(solution)/shard_map/all_to_all | solution.py:109
  356.3 100.1 %all-reduce.4 = (f32[8]{0:T(128)}, f32[8]{0:T(128)}) all-reduce(f32[8]{0:T(128)S(1)} %negate_multiply_fusion, f32[8]{0:T(128)S(1)} %get-tuple-element.385), channel_id=1, replica_groups=mesh['dp'=32,'tensor'=16] {'dp'}, use_global_device_ids=true, to_apply=%region_18.19 | all-reduce | flops 16 | bytes 128 | tf_op jit(solution)/shard_map/psum | solution.py:102
  457.1 2.3 copy.195
  (180 shorter events, 44.8 us)
Async XLA Ops:
  0.6 46.0 %copy-start.7 = (bf16[128,4096]{1,0:T(8,128)(2,1)S(1)}, bf16[128,4096]{1,0:T(8,128)(2,1)}, u32[]{:S(2)}) copy-start(bf16[128,4096]{1,0:T(8,128)(2,1)} %param.20) | copy-start | bytes 3145732
  2.2 14.4 %all-to-all-start.2 = ((bf16[128,16,8]{0,2,1:T(8,128)(2,1)}), bf16[128,16,8]{0,2,1:T(8,128)(2,1)S(1)}, u32[]{:S(2)}, u32[]{:S(2)}) async-start(bf16[128,16,8]{0,2,1:T(8,128)(2,1)} %bitcast.7), calls=%async_computation.2 | async-start | bytes 65536 | tf_op jit(solution)/shard_map/all_to_all | solution.py:76
  17.5 20.1 %all-to-all-start.1 = ((bf16[128,16,128]{0,2,1:T(8,128)(2,1)}), bf16[128,16,128]{0,2,1:T(8,128)(2,1)S(1)}, u32[]{:S(2)}, u32[]{:S(2)}) async-start(bf16[128,16,128]{0,2,1:T(8,128)(2,1)} %bitcast.3), calls=%async_computation.1 | async-start | bytes 1048576 | tf_op jit(solution)/shard_map/all_to_all | solution.py:78
  26.3 53.4 %copy-start.9 = (bf16[128,8,128]{2,1,0:T(8,128)(2,1)S(1)}, bf16[128,8,128]{2,1,0:T(8,128)(2,1)}, u32[]{:S(2)}) copy-start(bf16[128,8,128]{2,1,0:T(8,128)(2,1)} %param.15) | copy-start | bytes 786436
  37.6 24.3 %all-to-all-start.3 = ((bf16[128,16,256]{0,2,1:T(8,128)(2,1)}), bf16[128,16,256]{0,2,1:T(8,128)(2,1)S(1)}, u32[]{:S(2)}, u32[]{:S(2)}) async-start(bf16[128,16,256]{0,2,1:T(8,128)(2,1)} %bitcast.15), calls=%async_computation.3 | async-start | bytes 2097152 | tf_op jit(solution)/shard_map/all_to_all | solution.py:74
  61.9 33.0 %all-to-all-start = ((bf16[128,16,256]{0,2,1:T(8,128)(2,1)}), bf16[128,16,256]{0,2,1:T(8,128)(2,1)S(1)}, u32[]{:S(2)}, u32[]{:S(2)}) async-start(bf16[128,16,256]{0,2,1:T(8,128)(2,1)} %bitcast.271), calls=%async_computation | async-start | bytes 2097152 | tf_op jit(solution)/shard_map/all_to_all | solution.py:75
  79.7 3.8 copy-start.16
  81.9 13.1 %copy-start.6 = (bf16[128,8,128]{2,0,1:T(8,128)(2,1)S(1)}, bf16[128,8,128]{2,0,1:T(8,128)(2,1)}, u32[]{:S(2)}) copy-start(bf16[128,8,128]{2,0,1:T(8,128)(2,1)} %copy.171) | copy-start | bytes 786436
  94.9 1.2 copy-start.4
  96.1 30.9 %all-to-all-start.4 = ((bf16[128,16,128]{2,0,1:T(8,128)(2,1)}), bf16[128,16,128]{2,0,1:T(8,128)(2,1)S(1)}, u32[]{:S(2)}, u32[]{:S(2)}) async-start(bf16[128,16,128]{2,0,1:T(8,128)(2,1)} %bitcast.18), calls=%async_computation.4 | async-start | bytes 1048576 | tf_op jit(solution)/shard_map/all_to_all | solution.py:77
  117.1 67.3 %copy-start.13 = (f32[8,16,128]{2,1,0:T(8,128)}, f32[8,16,128]{2,1,0:T(8,128)S(1)}, u32[]{:S(2)}) copy-start(f32[8,16,128]{2,1,0:T(8,128)S(1)} %get-tuple-element.392) | copy-start | bytes 196612
  126.9 65.5 %copy-start = (bf16[2048,8,32]{0,2,1:T(8,128)(2,1)}, bf16[2048,8,32]{0,2,1:T(8,128)(2,1)S(1)}, u32[]{:S(2)}) copy-start(bf16[2048,8,32]{0,2,1:T(8,128)(2,1)S(1)} %reshape.164) | copy-start | bytes 3145732
  127.0 57.5 %copy-start.2 = (bf16[128,16,128]{2,0,1:T(8,128)(2,1)}, bf16[128,16,128]{2,0,1:T(8,128)(2,1)S(1)}, u32[]{:S(2)}) copy-start(bf16[128,16,128]{2,0,1:T(8,128)(2,1)S(1)} %all-to-all-done.4) | copy-start | bytes 1572868
  179.9 4.5 copy-start.3
  184.4 8.0 %copy-start.5 = (f32[16,8,32,128]{3,2,1,0:T(8,128)S(1)}, f32[16,8,32,128]{3,2,1,0:T(8,128)}, u32[]{:S(2)}) copy-start(f32[16,8,32,128]{3,2,1,0:T(8,128)} %get-tuple-element.525) | copy-start | bytes 6291460
  232.9 9.7 %copy-start.8 = (f32[8,16,128]{2,1,0:T(8,128)S(1)}, f32[8,16,128]{2,1,0:T(8,128)}, u32[]{:S(2)}) copy-start(f32[8,16,128]{2,1,0:T(8,128)} %get-tuple-element.398) | copy-start | bytes 196612
  232.9 9.7 %copy-start.10 = (f32[8,16,1]{2,1,0:T(8,128)S(1)}, f32[8,16,1]{2,1,0:T(8,128)}, u32[]{:S(2)}) copy-start(f32[8,16,1]{2,1,0:T(8,128)} %copy.189) | copy-start | bytes 1540
  232.9 9.7 %copy-start.11 = (f32[8,16,1]{2,1,0:T(8,128)S(1)}, f32[8,16,1]{2,1,0:T(8,128)}, u32[]{:S(2)}) copy-start(f32[8,16,1]{2,1,0:T(8,128)} %copy.188) | copy-start | bytes 1540
  255.7 21.3 %all-to-all-start.6 = ((f32[16,128,8]{1,2,0:T(8,128)}), f32[16,128,8]{1,2,0:T(8,128)S(1)}, u32[]{:S(2)}, u32[]{:S(2)}) async-start(f32[16,128,8]{1,2,0:T(8,128)} %get-tuple-element.390), calls=%async_computation.6 | async-start | bytes 131072 | tf_op jit(solution)/shard_map/all_to_all | solution.py:107
  265.3 9.5 %copy-start.1 = (bf16[2048,8,32]{0,2,1:T(8,128)(2,1)S(1)}, bf16[2048,8,32]{0,2,1:T(8,128)(2,1)}, u32[]{:S(2)}) copy-start(bf16[2048,8,32]{0,2,1:T(8,128)(2,1)} %copy-done) | copy-start | bytes 3145732
  265.3 9.5 %copy-start.15 = (f32[8]{0:T(128)S(1)}, f32[8]{0:T(128)}, u32[]{:S(2)}) copy-start(f32[8]{0:T(128)} %param.18) | copy-start | bytes 100
  275.5 11.5 %copy-start.12 = (f32[8,16,128]{2,1,0:T(8,128)S(1)}, f32[8,16,128]{2,1,0:T(8,128)}, u32[]{:S(2)}) copy-start(f32[8,16,128]{2,1,0:T(8,128)} %get-tuple-element.400) | copy-start | bytes 196612
  277.0 36.5 %all-to-all-start.5 = ((bf16[16,128,256]{1,2,0:T(8,128)(2,1)}), bf16[16,128,256]{1,2,0:T(8,128)(2,1)}, u32[]{:S(2)}, u32[]{:S(2)}) async-start(bf16[16,128,256]{1,2,0:T(8,128)(2,1)} %copy.181), calls=%async_computation.5 | async-start | bytes 2097152 | tf_op jit(solution)/shard_map/all_to_all | solution.py:103
  298.9 24.5 %copy-start.14 = (f32[8,16,128]{2,1,0:T(8,128)S(1)}, f32[8,16,128]{2,1,0:T(8,128)}, u32[]{:S(2)}) copy-start(f32[8,16,128]{2,1,0:T(8,128)} %copy-done.13) | copy-start | bytes 196612
  313.4 26.5 %all-to-all-start.7 = ((f32[2048,1,128]{2,1,0:T(1,128)}), f32[2048,1,128]{2,1,0:T(1,128)S(1)}, u32[]{:S(2)}, u32[]{:S(2)}) async-start(f32[2048,1,128]{2,1,0:T(1,128)} %bitcast.267), calls=%async_computation.7 | async-start | bytes 2097152 | tf_op jit(solution)/shard_map/all_to_all | solution.py:108
  340.0 120.3 %all-to-all-start.8 = ((f32[2048,1,128]{2,1,0:T(1,128)}), f32[2048,1,128]{2,1,0:T(1,128)S(1)}, u32[]{:S(2)}, u32[]{:S(2)}) async-start(f32[2048,1,128]{2,1,0:T(1,128)} %bitcast.47), calls=%async_computation.8 | async-start | bytes 2097152 | tf_op jit(solution)/shard_map/all_to_all | solution.py:109
where the time goes:
time: 470 us; the launch traced here: 462 us
  starting transfers between devices  109 us (23%)
  blocking collectives  100 us (21%)
  matrix products  96.8 us (21%)
  other arithmetic  73.9 us (16%)
  local copies, waits for them, and re-layouts  41 us (9%)
  waiting for transfers between devices  37.9 us (8%)
    psum x1, blocking collectives, on_device(): total_decay, total_skip = lax.psum((grad_decay, grad_skip), 'dp')  100 us
    dot_general x3, matrix products, head_forward(): jnp.einsum('cin,cjn->cij', out_c, in_c, precision=exact) * decay  36.8 us
    dot_general x3, matrix products, head_forward(): jnp.einsum('cjp,cjn->cpn', feat_c * weight_end[:, :, None], in_c, precisi...  28.2 us
    add x16, other arithmetic, advance(): return (made + reset * (coming - lax.stop_gradient(made)), state)  27.4 us
    reduce_sum x16, other arithmetic, advance(): made = factor * state + extra  17.9 us
    all_to_all x1, starting transfers between devices, on_device(): lax.all_to_all(grad_out, 'tensor', split_axis=1, concat_axis=0, tiled=True)  17.8 us
    all_to_all x1, starting transfers between devices, on_device(): lax.all_to_all(slot_in, 'tensor', split_axis=1, concat_axis=0, tiled=True)  17.8 us
    dot_general x2, matrix products, head_forward(): jnp.einsum('cin,cpn->cip', out_c * jnp.exp(cum)[:, :, None], entering, pr...  17.7 us
  transfers between devices with their start and end apart: 9, of which 4 were waited for; matrix products, arithmetic and copies ran while one was open for 17% of the time, Pallas kernels for 0%

commit v1 on v0

v1 whole, which is shorter than its diff:
```python
import functools

import jax
import jax.numpy as jnp
from jax import lax
from jax.experimental import pallas as pl
from jax.experimental.pallas import tpu as pltpu
from jax.sharding import PartitionSpec as P

MESH = pl.DeviceIdType.MESH
F32 = jnp.float32
BF16 = jnp.bfloat16
VMEM = pltpu.VMEM
LIMIT = 56 * 1024 * 1024

Q = 128
N = 128
PW = 32
HEADS = 128
GROUPS = 8
PER = HEADS // GROUPS
ROWS = PER * PW


def split2(x):
    hi = x.astype(BF16)
    return hi, (x - hi.astype(F32)).astype(BF16)


def split3(x):
    hi = x.astype(BF16)
    rest = x - hi.astype(F32)
    mid = rest.astype(BF16)
    return hi, mid, (rest - mid.astype(F32)).astype(BF16)


def mm(a, b, ca=1, cb=0):
    return lax.dot_general(a, b, (((ca,), (cb,)), ((), ())), preferred_element_type=F32)


def lane_sums(x, ones):
    return mm(jnp.concatenate(split3(x), axis=1), jnp.concatenate([ones] * 3, axis=0))


def iota(dim):
    return lax.broadcasted_iota(jnp.int32, (Q, Q), dim)


def expand(x):
    return jnp.broadcast_to(x[:, None, :], (x.shape[0], PW, x.shape[1])).reshape(-1, x.shape[1])


def head_sums(x):
    return x.reshape(-1, PW, x.shape[1]).sum(axis=1)


def peer_barrier(me, count):
    barrier = pltpu.get_barrier_semaphore()

    def greet(j, carry):
        peer = lax.rem(me + j, count)
        pl.semaphore_signal(barrier, inc=1, device_id={"tensor": peer}, device_id_type=MESH)
        return carry

    lax.fori_loop(1, count, greet, 0)
    pl.semaphore_wait(barrier, count - 1)


def prep_kernel(
    raw_ref, own_ref, x_ref, y_ref, b_ref, c_ref,
    cum_ref, v_ref, s_ref, sig_ref, a_ref, skip_ref, f_ref, xt_ref, yt_ref, d_ref, add_ref,
    gath, e_scr, w_scr, send_sem, recv_sem,
):
    me = lax.axis_index("tensor")
    count = gath.shape[0]
    peer_barrier(me, count)

    def copy_to(j):
        return pltpu.make_async_remote_copy(
            src_ref=own_ref, dst_ref=gath.at[me], send_sem=send_sem.at[j], recv_sem=recv_sem.at[j],
            device_id={"tensor": lax.rem(me + j, count)}, device_id_type=MESH,
        )

    def start(j, carry):
        copy_to(j).start()
        return carry

    def finish(j, carry):
        copy_to(j).wait()
        return carry

    lax.fori_loop(1, count, start, 0)
    gath[me] = own_ref[...]

    raw = raw_ref[...].astype(F32).T
    small = jnp.exp(-jnp.abs(raw))
    s = jnp.maximum(raw, 0.0) + jnp.log1p(small)
    sig_ref[...] = jnp.where(raw >= 0, 1.0, small) / (1.0 + small)
    s_ref[...] = s

    lax.fori_loop(1, count, finish, 0)
    a = jnp.exp(gath[:, 0:8, :].reshape(HEADS, Q))
    skip_ref[...] = gath[:, 8:16, :].reshape(HEADS, Q)
    a_ref[...] = a
    cum = lane_sums(-a * s, (iota(0) <= iota(1)).astype(F32).astype(BF16))
    last = jnp.broadcast_to(cum[:, Q - 1 : Q], (HEADS, Q))
    cum_ref[...] = cum
    v_ref[...] = cum - jnp.log(s)
    f_ref[...] = jnp.exp(last)
    e_scr[...] = jnp.exp(cum)
    w_scr[...] = jnp.exp(last - cum) * s

    def group(g, carry):
        lanes = pl.ds(pl.multiple_of(g * ROWS, ROWS), ROWS)
        heads = pl.ds(pl.multiple_of(g * PER, PER), PER)
        maps = pl.ds(pl.multiple_of(g * N, N), N)
        for src, dst, scale, m_ref, out in (
            (y_ref, yt_ref, e_scr, c_ref, d_ref),
            (x_ref, xt_ref, w_scr, b_ref, add_ref),
        ):
            turned = src[:, lanes].astype(F32).T
            dst[lanes, :] = turned.astype(BF16)
            hi, lo = split2(turned * expand(scale[heads, :]))
            m = m_ref[:, maps]
            out[lanes, :] = mm(jnp.concatenate([hi, lo], axis=1), jnp.concatenate([m, m], axis=0))
        return carry

    lax.fori_loop(0, GROUPS, group, 0)


def chain_kernel(
    d_ref, f_ref, add_ref, saved_ref,
    g_ref, e_ref,
    dsib, fsib, chain_in, chain_out, gsib_out, gsib_in, esaved, made_out, made_in,
    sems_s, sems_r,
):
    me = lax.axis_index("tensor")
    count = esaved.shape[0]
    core = lax.rem(me, 2)
    pair = me // 2
    pairs = count // 2
    sib = me + 1 - 2 * core
    half = count // 2
    peer_barrier(me, count)

    def rcopy(src, dst, s_sem, r_sem, dev):
        return pltpu.make_async_remote_copy(
            src_ref=src, dst_ref=dst, send_sem=s_sem, recv_sem=r_sem, device_id={"tensor": dev}, device_id_type=MESH
        )

    def d_copy(u):
        return rcopy(
            d_ref.at[(1 - core) * half + u], dsib.at[u], sems_s.at[u], sems_r.at[u], sib
        )

    def chain_copy(u):
        return rcopy(chain_out.at[u], chain_in.at[u], sems_s.at[16 + u], sems_r.at[16 + u], me - 2)

    def g_copy(u):
        return rcopy(gsib_out.at[u], gsib_in.at[u], sems_s.at[32 + u], sems_r.at[32 + u], sib)

    def saved_send(k):
        return rcopy(saved_ref.at[k - 1], esaved.at[me], sems_s.at[48 + k], sems_r.at[48 + me], 2 * k)

    def saved_recv(t):
        return rcopy(saved_ref.at[0], esaved.at[t], sems_s.at[48], sems_r.at[48 + t], sib)

    def made_copy(t):
        return rcopy(made_out.at[t], made_in.at[t], sems_s.at[64 + t], sems_r.at[64 + t], sib)

    f_copy = rcopy(f_ref, fsib, sems_s.at[80], sems_r.at[80], sib)

    def loop(lo, hi, body):
        def step(i, carry):
            body(i)
            return carry

        lax.fori_loop(lo, hi, step, 0)

    f_copy.start()
    loop(0, half, lambda u: d_copy(u).start())

    def send_saved(k):
        @pl.when(me != 2 * k)
        def _():
            saved_send(k).start()

        @pl.when(me == 2 * k)
        def _():
            esaved[me] = saved_ref[k - 1]

    loop(1, pairs, send_saved)

    f_copy.wait_recv()

    def chain_step(u):
        q = core * half + u
        heads = pl.ds(pl.multiple_of(q * 8, 8), 8)
        f_own, f_sib = f_ref[heads, :], fsib[heads, :]
        d_copy(u).wait_recv()
        d_own, d_sib = d_ref[q], dsib[u]
        even = core == 0
        d_even, d_odd = jnp.where(even, d_own, d_sib), jnp.where(even, d_sib, d_own)
        f_even, f_odd = jnp.where(even, f_own, f_sib), jnp.where(even, f_sib, f_own)
        f_odd = expand(f_odd)
        f_even = expand(f_even)

        @pl.when(pair < pairs - 1)
        def _():
            chain_copy(u).wait_recv()

        @pl.when(pair == pairs - 1)
        def _():
            chain_in[u] = jnp.zeros_like(d_own)

        coming = chain_in[u]
        to_even = d_odd + f_odd * coming

        @pl.when(pair > 0)
        def _():
            chain_out[u] = d_even + f_even * to_even
            chain_copy(u).start()

        g_ref[q] = jnp.where(even, to_even, coming)
        gsib_out[u] = jnp.where(even, coming, to_even)
        g_copy(u).start()

    loop(0, half, chain_step)

    def even_states(t):
        @pl.when(pair > 0)
        def _():
            @pl.when(t != me)
            def _():
                saved_recv(t).wait_recv()

            e_ref[t] = esaved[t].astype(F32)

        @pl.when(pair == 0)
        def _():
            e_ref[t] = jnp.zeros(e_ref.shape[1:], F32)

        heads = pl.ds(pl.multiple_of(t * 8, 8), 8)
        made_out[t] = expand(f_ref[heads, :]) * e_ref[t] + add_ref[t]
        made_copy(t).start()

    def odd_states(t):
        made_copy(t).wait_recv()
        e_ref[t] = made_in[t]

    @pl.when(core == 0)
    def _():
        loop(0, count, even_states)
        loop(0, count, lambda t: made_copy(t).wait_send())

    @pl.when(core == 1)
    def _():
        loop(0, count, odd_states)

    def sib_g(u):
        g_copy(u).wait()
        g_ref[(1 - core) * half + u] = gsib_in[u]
        d_copy(u).wait_send()

        @pl.when(pair > 0)
        def _():
            chain_copy(u).wait_send()

    loop(0, half, sib_g)
    f_copy.wait_send()

    def saved_sent(k):
        @pl.when(me != 2 * k)
        def _():
            saved_send(k).wait_send()

    loop(1, pairs, saved_sent)


def main_kernel(
    xt_ref, yt_ref, y_ref, b_ref, c_ref, cum_ref, v_ref, s_ref, sig_ref, a_ref, skip_ref, f_ref, e_ref, g_ref,
    dx_ref, draw_ref, db_ref, dc_ref, z_ref,
    dxt, u_scr, r_scr, draw_scr,
):
    g = pl.program_id(0)
    b, c = b_ref[...], c_ref[...]
    m = mm(c, b, 1, 1)
    cum, v, s = cum_ref[...], v_ref[...], s_ref[...]
    cum_n = cum.T
    inside = iota(0) >= iota(1)
    head_of = iota(0) // PW
    dm = jnp.zeros((Q, Q), F32)
    for q in range(PER // 4):
        rows = slice(q * Q, (q + 1) * Q)
        x4 = xt_ref[rows, :]
        wide = jnp.concatenate([jnp.where(head_of == h, x4.astype(F32), 0.0).astype(BF16) for h in range(4)], axis=1)
        ds4 = mm(y_ref[:, rows], wide)
        for h in range(4):
            hh = 4 * q + h
            mine = slice(q * Q + h * PW, q * Q + (h + 1) * PW)
            xh, yh = xt_ref[mine, :], yt_ref[mine, :]
            spread = cum_n[:, hh : hh + 1] - v[hh : hh + 1, :]
            decay = jnp.exp(jnp.where(inside, spread, -1e30))
            scores = m * decay
            dm = dm + ds4[:, h * Q : (h + 1) * Q] * decay
            both = jnp.concatenate(split2(scores), axis=0)
            dxw = mm(jnp.concatenate([yh, yh], axis=1), both)
            within = mm(xh, both, 1, 1)
            within = within[:, :Q] + within[:, Q:]
            dxt[mine, :] = dxw
            u_scr[hh : hh + 1, :] = jnp.sum(xh.astype(F32) * dxw, axis=0, keepdims=True)
            r_scr[hh : hh + 1, :] = jnp.sum(yh.astype(F32) * within, axis=0, keepdims=True)

    xt, yt = xt_ref[...].astype(F32), yt_ref[...].astype(F32)
    e_state, g_state = e_ref[...], g_ref[...]
    e_hi, e_lo = split2(e_state)
    g_hi, g_lo = split2(g_state)
    last = jnp.broadcast_to(cum[:, Q - 1 : Q], cum.shape)
    w = jnp.exp(last - cum) * s
    ex_w = expand(w)
    ey = expand(jnp.exp(cum)) * yt
    wx = ex_w * xt
    ec = mm(jnp.concatenate([e_hi, e_lo], axis=1), jnp.concatenate([c, c], axis=1), 1, 1)
    gb = mm(jnp.concatenate([g_hi, g_lo], axis=1), jnp.concatenate([b, b], axis=1), 1, 1)
    across = head_sums(ey * ec)
    ends = head_sums(wx * gb)

    dm_hi, dm_lo = split2(dm)
    ey_hi, ey_lo = split2(ey)
    wx_hi, wx_lo = split2(wx)
    dc = mm(jnp.concatenate([dm_hi, dm_lo], axis=1), jnp.concatenate([b, b], axis=0))
    dc = dc + mm(ey_hi, e_hi, 0, 0) + mm(ey_hi, e_lo, 0, 0) + mm(ey_lo, e_hi, 0, 0)
    dc_ref[...] = dc.astype(BF16)
    db = mm(jnp.concatenate([dm_hi, dm_lo], axis=0), jnp.concatenate([c, c], axis=0), 0, 0)
    db = db + mm(wx_hi, g_hi, 0, 0) + mm(wx_hi, g_lo, 0, 0) + mm(wx_lo, g_hi, 0, 0)
    db_ref[...] = db.astype(BF16)

    dx = dxt[...] + ex_w * gb + expand(skip_ref[...]) * yt
    dx_ref[...] = dx.T.astype(BF16)

    a, u, r = a_ref[...], u_scr[...], r_scr[...]
    through = jnp.sum(head_sums(e_state * g_state), axis=1, keepdims=True) * f_ref[...]
    at_end = through + jnp.sum(ends, axis=1, keepdims=True)
    lane = lax.broadcasted_iota(jnp.int32, (PER, Q), 1)
    dcum = r - u + across - ends + jnp.where(lane == Q - 1, at_end, 0.0)
    drate = lane_sums(dcum, (iota(0) >= iota(1)).astype(F32).astype(BF16))
    draw_scr[pl.ds(pl.multiple_of(g * PER, PER), PER), :] = (-a * drate + (u + ends) / s) * sig_ref[...]
    decay_part = jnp.sum(drate * (-a * s), axis=1, keepdims=True)
    skip_part = jnp.sum(head_sums(yt * xt), axis=1, keepdims=True)
    z_ref[...] = jnp.where(lane < Q // 2, decay_part, skip_part)

    @pl.when(g == GROUPS - 1)
    def _():
        draw_ref[...] = draw_scr[...].T


def total_kernel(dp_inner, z_ref, out_ref, part, from_t, from_i, from_o, send_sem, recv_sem):
    me = lax.axis_index("tensor")
    row = lax.axis_index("dp")
    n_t = from_t.shape[0]
    n_i, n_o = from_i.shape[0], from_o.shape[0]
    inner, outer = lax.rem(row, dp_inner), row // dp_inner

    def loop(lo, hi, body):
        def step(i, carry):
            body(i)
            return carry

        lax.fori_loop(lo, hi, step, 0)

    def dev_t(j):
        return {"tensor": lax.rem(me + j, n_t)}

    def dev_i(j):
        return {"dp": outer * dp_inner + lax.rem(inner + j, n_i)}

    def dev_o(j):
        return {"dp": lax.rem(outer + j, n_o) * dp_inner + inner}

    barrier = pltpu.get_barrier_semaphore()
    for n, dev in ((n_t, dev_t), (n_i, dev_i), (n_o, dev_o)):
        loop(1, n, lambda j: pl.semaphore_signal(barrier, inc=1, device_id=dev(j), device_id_type=MESH))
    pl.semaphore_wait(barrier, n_t - 1 + n_i - 1 + n_o - 1)

    def exchange(n, dev, at, source, landing, base):
        def copy(j):
            return pltpu.make_async_remote_copy(
                src_ref=source(j), dst_ref=landing.at[at],
                send_sem=send_sem.at[base + j], recv_sem=recv_sem.at[base + j],
                device_id=dev(j), device_id_type=MESH,
            )

        loop(1, n, lambda j: copy(j).start())
        landing[at] = source(0)[...]
        loop(1, n, lambda j: copy(j).wait())
        return jnp.sum(landing[...], axis=0)

    part[0] = exchange(n_t, dev_t, me, lambda j: z_ref.at[lax.rem(me + j, n_t)], from_t, 0)
    part[1] = exchange(n_i, dev_i, inner, lambda j: part.at[0], from_i, n_t)
    out_ref[...] = exchange(n_o, dev_o, outer, lambda j: part.at[1], from_o, n_t + n_i)


def on_device(features, step_raw, input_map, output_map, decay_log, skip_gain, saved_states, grad_out):
    n_t = lax.axis_size("tensor")
    n_dp = lax.axis_size("dp")
    b = input_map.reshape(Q, GROUPS * N)
    c = output_map.reshape(Q, GROUPS * N)
    own = jnp.broadcast_to(jnp.concatenate([decay_log, skip_gain])[:, None], (16, Q))
    table = jax.ShapeDtypeStruct((HEADS, Q), F32)
    turned = jax.ShapeDtypeStruct((HEADS * PW, Q), BF16)
    states = jax.ShapeDtypeStruct((HEADS * PW, N), F32)
    whole = pl.BlockSpec(memory_space=VMEM)

    def params(cid=None):
        if cid is None:
            return pltpu.CompilerParams(vmem_limit_bytes=LIMIT)
        return pltpu.CompilerParams(vmem_limit_bytes=LIMIT, collective_id=cid, has_side_effects=True)

    cum, v, s, sig, a, skip, f, xt, yt, d, add = pl.pallas_call(
        prep_kernel,
        out_shape=[table] * 7 + [turned] * 2 + [states] * 2,
        in_specs=[whole] * 6,
        out_specs=[whole] * 11,
        scratch_shapes=[
            VMEM((n_t, 16, Q), F32), VMEM((HEADS, Q), F32), VMEM((HEADS, Q), F32),
            pltpu.SemaphoreType.DMA((n_t,)), pltpu.SemaphoreType.DMA((n_t,)),
        ],
        compiler_params=params(0),
        name="prep",
    )(step_raw, own, features, grad_out, b, c)

    chunk = HEADS * PW // n_t
    half = n_t // 2
    chunks = jax.ShapeDtypeStruct((n_t, chunk, N), F32)
    halves = VMEM((half, chunk, N), F32)
    g_state, e_state = pl.pallas_call(
        chain_kernel,
        out_shape=[chunks, chunks],
        in_specs=[whole] * 4,
        out_specs=[whole] * 2,
        scratch_shapes=[
            halves, VMEM((HEADS, Q), F32), halves, halves, halves, halves,
            VMEM((n_t, chunk, N), BF16), VMEM((n_t, chunk, N), F32), VMEM((n_t, chunk, N), F32),
            pltpu.SemaphoreType.DMA((81,)), pltpu.SemaphoreType.DMA((81,)),
        ],
        compiler_params=params(1),
        name="chain",
    )(d.reshape(chunks.shape), f, add.reshape(chunks.shape), saved_states.reshape(-1, chunk, N))

    by_head = pl.BlockSpec((PER, Q), lambda g: (g, 0))
    by_row = pl.BlockSpec((ROWS, Q), lambda g: (g, 0))
    by_map = pl.BlockSpec((Q, N), lambda g: (0, g))
    by_lane = pl.BlockSpec((Q, ROWS), lambda g: (0, g))
    dx, draw, db, dc, z = pl.pallas_call(
        main_kernel,
        grid=(GROUPS,),
        out_shape=[
            jax.ShapeDtypeStruct((Q, HEADS * PW), BF16),
            jax.ShapeDtypeStruct((Q, HEADS), F32),
            jax.ShapeDtypeStruct((Q, GROUPS * N), BF16),
            jax.ShapeDtypeStruct((Q, GROUPS * N), BF16),
            table,
        ],
        in_specs=[by_row, by_row, by_lane, by_map, by_map] + [by_head] * 7 + [by_row] * 2,
        out_specs=[by_lane, pl.BlockSpec((Q, HEADS), lambda g: (0, 0)), by_map, by_map, by_head],
        scratch_shapes=[VMEM((ROWS, Q), F32), VMEM((PER, Q), F32), VMEM((PER, Q), F32), VMEM((HEADS, Q), F32)],
        compiler_params=params(),
        name="main",
    )(xt, yt, grad_out, b, c, cum, v, s, sig, a, skip, f, e_state.reshape(states.shape), g_state.reshape(states.shape))

    dp_inner = 8 if n_dp % 8 == 0 else n_dp
    dp_outer = n_dp // dp_inner
    sums = n_t + dp_inner + dp_outer
    total = pl.pallas_call(
        functools.partial(total_kernel, dp_inner),
        out_shape=jax.ShapeDtypeStruct((8, Q), F32),
        in_specs=[whole],
        out_specs=whole,
        scratch_shapes=[
            VMEM((2, 8, Q), F32),
            VMEM((n_t, 8, Q), F32), VMEM((dp_inner, 8, Q), F32), VMEM((dp_outer, 8, Q), F32),
            pltpu.SemaphoreType.DMA((sums,)), pltpu.SemaphoreType.DMA((sums,)),
        ],
        compiler_params=params(2),
        name="total",
    )(z.reshape(n_t, 8, Q))
    return (
        dx,
        draw,
        db.reshape(Q, GROUPS, N),
        dc.reshape(Q, GROUPS, N),
        total[:, 0],
        total[:, Q // 2],
    )


def solution(mesh):
    placed = (
        P(("dp", "tensor"), None),
        P(("dp", "tensor"), None),
        P(("dp", "tensor"), None, None),
        P(("dp", "tensor"), None, None),
        P("tensor"),
        P("tensor"),
        P("dp", None, "tensor", None, None),
        P(("dp", "tensor"), None),
    )
    return jax.shard_map(
        on_device,
        mesh=mesh,
        in_specs=placed,
        out_specs=(
            P(("dp", "tensor"), None),
            P(("dp", "tensor"), None),
            P(("dp", "tensor"), None, None),
            P(("dp", "tensor"), None, None),
            P("tensor"),
            P("tensor"),
        ),
        check_vma=False,
    )
```

time: 470 us -> 167 us (0.36)
  the two profiles are of different devices: /device:TPU:32 before, /device:TPU:1 now
where the time goes in v1:
time: 167 us
  Pallas kernels  158 us (95%)
  local copies, waits for them, and re-layouts  7.46 us (4%)
    pallas_call x1, Pallas kernels, on_device(): pl.pallas_call(chain_kernel, out_shape=[chunks, chunks], in_specs=[whole]...  75.9 us
    pallas_call x1, Pallas kernels, on_device(): pl.pallas_call(functools.partial(total_kernel, dp_inner), out_shape=jax.S...  42.5 us
    pallas_call x1, Pallas kernels, on_device(): pl.pallas_call(prep_kernel, out_shape=[table] * 7 + [turned] * 2 + [state...  25.1 us
    pallas_call x1, Pallas kernels, on_device(): pl.pallas_call(main_kernel, grid=(GROUPS,), out_shape=[jax.ShapeDtypeStru...  14.5 us
    unnamed x2, local copies, waits for them, and re-layouts  3.4 us

profile of v1, /device:TPU:1, one launch (start us, length us, event | category | flops | bytes accessed | tf_op | source)
XLA Modules:
  0.0 166.8 jit_solution(7285469542169239317)
XLA Ops:
  0.6 0.7 pad_maximum_fusion
  1.4 0.7 broadcast_in_dim.2.own_ref
  2.1 1.9 %copy_bitcast_fusion = (bf16[128,1024]{1,0:T(8,128)(2,1)}, bf16[128,1024]{1,0:T(8,128)(2,1)}) fusion(bf16[16,8,8,128]{3,2,1,0:T(8,128)(2,1)} %bitcast.25, bf16[16,8,8,128]{3,2,1,0:T(8,128)(2,1)} %bitcast.26), kind=kLoop, calls=%fused_computation | loop fusion | bytes 1048576 | tf_op jit(solution)/shard_map/reshape | solution.py:407
  4.0 25.1 %prep.1 = (f32[128,128]{1,0:T(8,128)}, f32[128,128]{1,0:T(8,128)}, f32[128,128]{1,0:T(8,128)}, f32[128,128]{1,0:T(8,128)}, f32[128,128]{1,0:T(8,128)}, /*index=5...) custom-call(bf16[128,128]{1,0:T(8,128)(2,1)} %raw_ref.1, ...), custom_call_target="tpu_custom_call" | custom-call | tf_op jit(solution)/shard_map/prep/pallas_call | solution.py:419
  29.0 75.9 %chain.1 = (f32[16,256,128]{2,1,0:T(8,128)}, f32[16,256,128]{2,1,0:T(8,128)}) custom-call(f32[16,256,128]{2,1,0:T(8,128)} %bitcast.16, f32[128,128]{1,0:T(8,128)} %get-tuple-element.32.f_ref, f32[16,256,128]{2,1,0:T(8,128)} %bitcast.17, bf16[7,256,128]{2,1,0:T(8,128)(2,1)} %bitcast.20), custom_call_target="tpu_custom_call" | custom-call | tf_op jit(solution)/shard_map/chain/pallas_call | solution.py:436
  105.0 14.5 %main.1 = (bf16[128,4096]{1,0:T(8,128)(2,1)}, f32[128,128]{1,0:T(8,128)}, bf16[128,1024]{1,0:T(8,128)(2,1)}, bf16[128,1024]{1,0:T(8,128)(2,1)}, f32[128,128]{1,0:T(8,128)}) custom-call(bf16[4096,128]{1,0:T(8,128)(2,1)} %get-tuple-element.24.xt_ref, bf16[4096,128]{1,0:T(8,128)(2,1)} %get-tuple-element.25.yt_ref, bf16[128,4096]{1,0:T(8,128)(2,1)} %y_ref.3, ...), custom_call_target="tpu_custom_call" | custom-call | tf_op jit(solution)/shard_map/main/pallas_call | solution.py:454
  119.4 42.5 %total.1 = f32[8,128]{1,0:T(8,128)} custom-call(f32[16,8,128]{2,1,0:T(8,128)} %bitcast.27), custom_call_target="tpu_custom_call" | custom-call | tf_op jit(solution)/shard_map/total/pallas_call | solution.py:474
  161.9 1.5 slice_reduce_fusion
  163.4 1.7 %copy.16 = bf16[16,8,8,128]{3,2,1,0:T(8,128)(2,1)} copy(bf16[16,8,8,128]{3,1,2,0:T(8,128)(2,1)} %bitcast.22) | data formatting | bytes 524288
  165.1 1.7 %copy.17 = bf16[16,8,8,128]{3,2,1,0:T(8,128)(2,1)} copy(bf16[16,8,8,128]{3,1,2,0:T(8,128)(2,1)} %bitcast.21) | data formatting | bytes 524288

commit v2 on v0

v2 whole, which is shorter than its diff:
```python
import functools

import jax
import jax.numpy as jnp
from jax import lax
from jax.experimental import pallas as pl
from jax.experimental.pallas import tpu as pltpu
from jax.sharding import PartitionSpec as P

MESH = pl.DeviceIdType.MESH
F32 = jnp.float32
BF16 = jnp.bfloat16
VMEM = pltpu.VMEM
LIMIT = 56 * 1024 * 1024

Q = 128
N = 128
PW = 32
HEADS = 128
GROUPS = 8
PER = HEADS // GROUPS
ROWS = PER * PW


def split2(x):
    hi = x.astype(BF16)
    return hi, (x - hi.astype(F32)).astype(BF16)


def split3(x):
    hi = x.astype(BF16)
    rest = x - hi.astype(F32)
    mid = rest.astype(BF16)
    return hi, mid, (rest - mid.astype(F32)).astype(BF16)


def mm(a, b, ca=1, cb=0):
    return lax.dot_general(a, b, (((ca,), (cb,)), ((), ())), preferred_element_type=F32)


def lane_sums(x, ones):
    return mm(jnp.concatenate(split3(x), axis=1), jnp.concatenate([ones] * 3, axis=0))


def iota(dim):
    return lax.broadcasted_iota(jnp.int32, (Q, Q), dim)


def expand(x):
    return jnp.broadcast_to(x[:, None, :], (x.shape[0], PW, x.shape[1])).reshape(-1, x.shape[1])


def head_sums(x):
    return x.reshape(-1, PW, x.shape[1]).sum(axis=1)

CHIPS = 4
SUBS = 4
SUB = ROWS // SUBS
HEADS_SUB = PER // SUBS
WIRE = SUB + 8


def loop(lo, hi, body):
    def step(i, carry):
        body(i)
        return carry

    lax.fori_loop(lo, hi, step, 0)


def spans(i, size):
    return pl.ds(pl.multiple_of(i * size, size), size)


def kernel(
    dp_inner,
    raw_ref, own_ref, x_ref, y_ref, b_ref, c_ref, saved_ref,
    dx_ref, draw_ref, db_ref, dc_ref, total_ref,
    gath, cum_s, v_s, s_s, sig_s, a_s, skip_s, f_s, e_s, w_s, fsib, u_s, r_s, drate_s, z_s,
    bm, cm, wide_f32, xt, yt, d_s, dsib, comp, cin, rout, yout, yin, rin, gst, gout,
    esaved, est, mout, dxt, db_acc, dc_acc,
    part, from_t, from_i, from_o,
    own_sem, saved_sem, f_sem, d_sem, in_sem, y_sem, ret_sem, g_sem, made_sem, sum_sem,
):
    me = lax.axis_index("tensor")
    rep = lax.axis_index("dp")
    n_t, n_i, n_o = from_t.shape[0], from_i.shape[0], from_o.shape[0]
    core = lax.rem(me, 2)
    even = core == 0
    pair = me // 2
    x = lax.rem(pair, CHIPS)
    row = pair // CHIPS
    sib = me + 1 - 2 * core
    inner, outer = lax.rem(rep, dp_inner), rep // dp_inner
    last_pair = pair == n_t // 2 - 1

    def dev_t(j):
        return {"tensor": lax.rem(me + j, n_t)}

    def dev_i(j):
        return {"dp": outer * dp_inner + lax.rem(inner + j, n_i)}

    def dev_o(j):
        return {"dp": lax.rem(outer + j, n_o) * dp_inner + inner}

    def remote(src, dst, sems, i, j, dev):
        return pltpu.make_async_remote_copy(
            src_ref=src, dst_ref=dst, send_sem=sems.at[(0, *i)], recv_sem=sems.at[(1, *j)],
            device_id=dev, device_id_type=MESH,
        )

    barrier = pltpu.get_barrier_semaphore()
    for n, dev in ((n_t, dev_t), (n_i, dev_i), (n_o, dev_o)):
        loop(1, n, lambda j: pl.semaphore_signal(barrier, inc=1, device_id=dev(j), device_id_type=MESH))
    pl.semaphore_wait(barrier, n_t - 1 + n_i - 1 + n_o - 1)

    def own_copy(j):
        return remote(own_ref, gath.at[me], own_sem, (j,), (j,), dev_t(j))

    def saved_copy(k):
        return remote(saved_ref.at[k - 1], esaved.at[me], saved_sem, (k,), (me,), {"tensor": 2 * k})

    def saved_arrival(t):
        return remote(saved_ref.at[0], esaved.at[t], saved_sem, (0,), (t,), {"tensor": sib})

    def send_saved(k):
        @pl.when(me != 2 * k)
        def _():
            saved_copy(k).start()

        @pl.when(me == 2 * k)
        def _():
            esaved[me] = saved_ref[k - 1]

    loop(1, n_t, lambda j: own_copy(j).start())
    loop(1, n_t // 2, send_saved)
    gath[me] = own_ref[...]

    raw = raw_ref[...].astype(F32).T
    small = jnp.exp(-jnp.abs(raw))
    s = jnp.maximum(raw, 0.0) + jnp.log1p(small)
    sig_s[...] = (jnp.where(raw >= 0, 1.0, small) / (1.0 + small)).reshape(sig_s.shape)
    s_s[...] = s.reshape(s_s.shape)
    for src, dst in ((b_ref, bm), (c_ref, cm)):
        wide_f32[...] = src[...].astype(F32)
        for g in range(GROUPS):
            dst[g] = wide_f32[pl.ds(g, Q, stride=GROUPS), :].astype(BF16)

    def turn(g):
        for src, dst in ((y_ref, yt), (x_ref, xt)):
            dst[g] = src[:, spans(g, ROWS)].astype(F32).T.astype(BF16)

    loop(0, GROUPS, turn)

    loop(1, n_t, lambda j: own_copy(j).wait())
    a = jnp.exp(gath[:, 0:8, :].reshape(HEADS, Q))
    skip_s[...] = gath[:, 8:16, :].reshape(skip_s.shape)
    a_s[...] = a.reshape(a_s.shape)
    cum = lane_sums(-a * s, (iota(0) <= iota(1)).astype(F32).astype(BF16))
    last = jnp.broadcast_to(cum[:, Q - 1 : Q], (HEADS, Q))
    cum_s[...] = cum.reshape(cum_s.shape)
    v_s[...] = (cum - jnp.log(s)).reshape(v_s.shape)
    f_s[...] = jnp.exp(last).reshape(f_s.shape)
    e_s[...] = jnp.exp(cum).reshape(e_s.shape)
    w_s[...] = (jnp.exp(last - cum) * s).reshape(w_s.shape)
    f_copy = remote(f_s, fsib, f_sem, (0,), (0,), {"tensor": sib})
    f_copy.start()

    def d_copy(q):
        return remote(d_s.at[2 * q + 1 - core], dsib.at[q], d_sem, (q,), (q,), {"tensor": sib})

    def made_of(g):
        hi, lo = split2(yt[g].astype(F32) * expand(e_s[g]))
        m = cm[g]
        both = mm(jnp.concatenate([hi, lo], axis=1), jnp.concatenate([m, m], axis=0))
        d_s[g] = both.reshape(SUBS, SUB, N)

    def first_half(q):
        made_of(2 * q + 1 - core)
        d_copy(q).start()

    loop(0, CHIPS, first_half)
    loop(0, CHIPS, lambda q: made_of(2 * q + core))

    def in_copy(q, t):
        return remote(
            comp.at[q, t], cin.at[x, t], in_sem, (q, t), (x, t), {"tensor": row * 2 * CHIPS + 2 * q + core}
        )

    def in_arrival(j, t):
        return remote(comp.at[j, t], cin.at[j, t], in_sem, (j, t), (j, t), {"tensor": sib})

    f_copy.wait()

    def fold(q):
        g = 2 * q + core
        f_own, f_sib = f_s[g], fsib[g]
        f_even, f_odd = jnp.where(even, f_own, f_sib), jnp.where(even, f_sib, f_own)
        d_copy(q).wait_recv()
        for t in range(SUBS):
            hs = slice(t * HEADS_SUB, (t + 1) * HEADS_SUB)
            d_own, d_sib = d_s[g, t], dsib[q, t]
            d_even, d_odd = jnp.where(even, d_own, d_sib), jnp.where(even, d_sib, d_own)
            comp[q, t, 0:SUB, :] = d_even + expand(f_even[hs]) * d_odd
            f_both = (f_even * f_odd)[hs]
            comp[q, t, SUB:WIRE, :] = jnp.concatenate([f_both, f_both], axis=0)

        @pl.when(q != x)
        def _():
            for t in range(SUBS):
                in_copy(q, t).start()

        @pl.when(q == x)
        def _():
            cin[x] = comp[q]

    loop(0, CHIPS, fold)

    inside = iota(0) >= iota(1)
    head_of = iota(0) // PW

    def local(g):
        b, c = bm[g], cm[g]
        m = mm(c, b, 1, 1)
        v = v_s[g]
        cum_n = cum_s[g].T
        dm = jnp.zeros((Q, Q), F32)
        for q in range(PER // 4):
            x4 = xt[g, q * Q : (q + 1) * Q, :].astype(F32)
            wide = jnp.concatenate([jnp.where(head_of == h, x4, 0.0).astype(BF16) for h in range(4)], axis=1)
            y4 = y_ref[:, pl.ds(pl.multiple_of(g * ROWS + q * Q, Q), Q)]
            ds4 = mm(y4, wide)
            for h in range(4):
                hh = 4 * q + h
                mine = slice(hh * PW, (hh + 1) * PW)
                xh, yh = xt[g, mine, :], yt[g, mine, :]
                spread = cum_n[:, hh : hh + 1] - v[hh : hh + 1, :]
                decay = jnp.exp(jnp.where(inside, spread, -1e30))
                scores = m * decay
                dm = dm + ds4[:, h * Q : (h + 1) * Q] * decay
                both = jnp.concatenate(split2(scores), axis=0)
                dxw = mm(jnp.concatenate([yh, yh], axis=1), both)
                within = mm(xh, both, 1, 1)
                within = within[:, :Q] + within[:, Q:]
                dxt[g, mine, :] = dxw
                u_s[g, hh : hh + 1, :] = jnp.sum(xh.astype(F32) * dxw, axis=0, keepdims=True)
                r_s[g, hh : hh + 1, :] = jnp.sum(yh.astype(F32) * within, axis=0, keepdims=True)
        dm_hi, dm_lo = split2(dm)
        dc_acc[g] = mm(jnp.concatenate([dm_hi, dm_lo], axis=1), jnp.concatenate([b, b], axis=0))
        db_acc[g] = mm(jnp.concatenate([dm_hi, dm_lo], axis=0), jnp.concatenate([c, c], axis=0), 0, 0)

    loop(0, GROUPS // 2, local)

    def y_copy(t):
        return remote(yout.at[t], yin.at[t], y_sem, (t,), (t,), {"tensor": me - row * 2 * CHIPS})

    def ret_copy(j, t):
        return remote(
            rout.at[j, t], rin.at[x, t], ret_sem, (j, t), (x, t), {"tensor": row * 2 * CHIPS + 2 * j + core}
        )

    def ret_arrival(q, t):
        return remote(rout.at[q, t], rin.at[q, t], ret_sem, (q, t), (q, t), {"tensor": sib})

    def hand_back(j, t):
        @pl.when(j != x)
        def _():
            ret_copy(j, t).start()

        @pl.when(j == x)
        def _():
            rin[x, t] = rout[j, t]

    def factor(j, t):
        return cin[j, t, SUB : SUB + HEADS_SUB, :]

    for t in range(SUBS):
        for j in range(CHIPS):

            @pl.when(j != x)
            def _():
                in_arrival(j, t).wait_recv()

        state = cin[CHIPS - 1, t, 0:SUB, :]
        for j in range(CHIPS - 2, -1, -1):
            rout[j, t] = state
            state = cin[j, t, 0:SUB, :] + expand(factor(j, t)) * state
        yout[t] = state

        @pl.when(row == 1)
        def _():
            y_copy(t).start()
            for j in range(CHIPS - 1):
                hand_back(j, t)

    @pl.when(last_pair)
    def _():
        rin[...] = jnp.zeros(rin.shape, F32)

    loop(GROUPS // 2, GROUPS, local)

    def made_copy(g):
        return remote(mout.at[g], est.at[g], made_sem, (g,), (g,), {"tensor": sib})

    def even_states(g):
        @pl.when(pair > 0)
        def _():
            for i in range(2):
                t = 2 * g + i

                @pl.when(t != me)
                def _():
                    saved_arrival(t).wait_recv()

                est[g, i] = esaved[t].astype(F32)

        @pl.when(pair == 0)
        def _():
            est[g] = jnp.zeros(est.shape[1:], F32)

        hi, lo = split2(xt[g].astype(F32) * expand(w_s[g]))
        m = bm[g]
        added = mm(jnp.concatenate([hi, lo], axis=1), jnp.concatenate([m, m], axis=0))
        mout[g] = (expand(f_s[g]) * est[g].reshape(ROWS, N) + added).reshape(mout.shape[1:])
        made_copy(g).start()

    @pl.when(even)
    def _():
        loop(0, GROUPS, even_states)

    @pl.when(row == 0)
    def _():
        for t in range(SUBS):
            y_copy(t).wait_recv()
            coming = yin[t]
            rout[CHIPS - 1, t] = coming
            through = factor(CHIPS - 1, t)
            for j in range(CHIPS - 2, -1, -1):
                rout[j, t] = rout[j, t] + expand(through) * coming
                through = through * factor(j, t)
            for j in range(CHIPS):
                hand_back(j, t)

    def from_states(g):
        @pl.when(core == 1)
        def _():
            made_copy(g).wait_recv()

        e_state = est[g].reshape(ROWS, N)
        e_hi, e_lo = split2(e_state)
        c = cm[g]
        ey = expand(e_s[g]) * yt[g].astype(F32)
        ey_hi, ey_lo = split2(ey)
        ec = mm(jnp.concatenate([e_hi, e_lo], axis=1), jnp.concatenate([c, c], axis=1), 1, 1)
        r_s[g] = r_s[g] + head_sums(ey * ec)
        dc_acc[g] = dc_acc[g] + mm(ey_hi, e_hi, 0, 0) + mm(ey_hi, e_lo, 0, 0) + mm(ey_lo, e_hi, 0, 0)

    loop(0, GROUPS, from_states)

    def g_copy(q, t):
        g = 2 * q + core
        return remote(gout.at[q, t], gst.at[g, t], g_sem, (q, t), (q, t), {"tensor": sib})

    def own_gradient(q):
        g = 2 * q + core
        f_odd = jnp.where(even, fsib[g], f_s[g])
        for t in range(SUBS):

            @pl.when(jnp.logical_and(q != x, jnp.logical_not(last_pair)))
            def _():
                ret_arrival(q, t).wait_recv()

            coming = rin[q, t]
            d_odd = jnp.where(even, dsib[q, t], d_s[g, t])
            to_even = d_odd + expand(f_odd[t * HEADS_SUB : (t + 1) * HEADS_SUB]) * coming
            gst[g, t] = jnp.where(even, to_even, coming)
            gout[q, t] = jnp.where(even, coming, to_even)
            g_copy(q, t).start()

    loop(0, CHIPS, own_gradient)

    lane = lax.broadcasted_iota(jnp.int32, (PER, Q), 1)

    def from_gradient(g):
        b = bm[g]
        g_state = gst[g].reshape(ROWS, N)
        g_hi, g_lo = split2(g_state)
        gb = mm(jnp.concatenate([g_hi, g_lo], axis=1), jnp.concatenate([b, b], axis=1), 1, 1)
        xf, yf = xt[g].astype(F32), yt[g].astype(F32)
        ex_w = expand(w_s[g])
        wx = ex_w * xf
        wx_hi, wx_lo = split2(wx)
        ends = head_sums(wx * gb)
        db_acc[g] = db_acc[g] + mm(wx_hi, g_hi, 0, 0) + mm(wx_hi, g_lo, 0, 0) + mm(wx_lo, g_hi, 0, 0)
        dx = dxt[g] + ex_w * gb + expand(skip_s[g]) * yf
        dx_ref[:, spans(g, ROWS)] = dx.T.astype(BF16)
        a, sg = a_s[g], s_s[g]
        e_state = est[g].reshape(ROWS, N)
        through = jnp.sum(head_sums(e_state * g_state), axis=1, keepdims=True) * f_s[g]
        at_end = through + jnp.sum(ends, axis=1, keepdims=True)
        u = u_s[g]
        dcum = r_s[g] - u - ends + jnp.where(lane == Q - 1, at_end, 0.0)
        drate = lane_sums(dcum, (iota(0) >= iota(1)).astype(F32).astype(BF16))
        drate_s[g] = (-a * drate + (u + ends) / sg) * sig_s[g]
        decay_part = jnp.sum(drate * (-a * sg), axis=1, keepdims=True)
        skip_part = jnp.sum(head_sums(yf * xf), axis=1, keepdims=True)
        z_s[g] = jnp.where(lane < Q // 2, decay_part, skip_part)

    loop(0, CHIPS, lambda q: from_gradient(2 * q + core))

    def sibs_gradient(q):
        for t in range(SUBS):
            g_copy(q, t).wait_recv()
        from_gradient(2 * q + 1 - core)

    loop(0, CHIPS, sibs_gradient)

    def exchange(n, dev, at, source, landing, base, beside):
        def copy(j):
            return remote(source(j), landing.at[at], sum_sem, (base + j,), (base + j,), dev(j))

        loop(1, n, lambda j: copy(j).start())
        landing[at] = source(0)[...]
        beside()
        loop(1, n, lambda j: copy(j).wait())
        return jnp.sum(landing[...], axis=0)

    def z_part(j):
        t = lax.rem(me + j, n_t)
        return z_s.at[t // 2, spans(lax.rem(t, 2), 8), :]

    def write_maps(acc, out):
        for g in range(GROUPS):
            wide_f32[pl.ds(g, Q, stride=GROUPS), :] = acc[g]
        out[...] = wide_f32[...].astype(BF16)

    def write_step():
        draw_ref[...] = drate_s[...].reshape(HEADS, Q).T

    part[0] = exchange(n_t, dev_t, me, z_part, from_t, 0, lambda: write_maps(db_acc, db_ref))
    part[1] = exchange(n_i, dev_i, inner, lambda j: part.at[0], from_i, n_t, lambda: write_maps(dc_acc, dc_ref))
    total_ref[...] = exchange(n_o, dev_o, outer, lambda j: part.at[1], from_o, n_t + n_i, write_step)

    def sent_saved(k):
        @pl.when(me != 2 * k)
        def _():
            saved_copy(k).wait_send()

    loop(1, n_t // 2, sent_saved)

    def sent(q):
        d_copy(q).wait_send()
        for t in range(SUBS):
            g_copy(q, t).wait_send()

            @pl.when(q != x)
            def _():
                in_copy(q, t).wait_send()

                @pl.when(jnp.logical_or(row == 0, q < CHIPS - 1))
                def _():
                    ret_copy(q, t).wait_send()

    loop(0, CHIPS, sent)

    @pl.when(row == 1)
    def _():
        for t in range(SUBS):
            y_copy(t).wait_send()

    @pl.when(even)
    def _():
        loop(0, GROUPS, lambda g: made_copy(g).wait_send())


def on_device(features, step_raw, input_map, output_map, decay_log, skip_gain, saved_states, grad_out):
    n_t = lax.axis_size("tensor")
    n_dp = lax.axis_size("dp")
    own = jnp.broadcast_to(jnp.concatenate([decay_log, skip_gain])[:, None], (16, Q))
    whole = pl.BlockSpec(memory_space=VMEM)
    dp_inner = 8 if n_dp % 8 == 0 else n_dp
    dp_outer = n_dp // dp_inner
    sums = n_t + dp_inner + dp_outer
    table = VMEM((GROUPS, PER, Q), F32)
    turned = VMEM((GROUPS, ROWS, Q), BF16)
    states = VMEM((GROUPS, SUBS, SUB, N), F32)
    quarters = VMEM((CHIPS, SUBS, SUB, N), F32)
    wires = VMEM((CHIPS, SUBS, WIRE, N), F32)
    eighth = VMEM((SUBS, SUB, N), F32)
    chunk = HEADS * PW // n_t
    halves = VMEM((GROUPS, 2, chunk, N), F32)
    maps = VMEM((GROUPS, Q, N), F32)
    sems = pltpu.SemaphoreType.DMA
    dx, draw, db, dc, total = pl.pallas_call(
        functools.partial(kernel, dp_inner),
        out_shape=[
            jax.ShapeDtypeStruct((Q, HEADS * PW), BF16),
            jax.ShapeDtypeStruct((Q, HEADS), F32),
            jax.ShapeDtypeStruct((Q * GROUPS, N), BF16),
            jax.ShapeDtypeStruct((Q * GROUPS, N), BF16),
            jax.ShapeDtypeStruct((8, Q), F32),
        ],
        in_specs=[whole] * 7,
        out_specs=[whole] * 5,
        scratch_shapes=[
            VMEM((n_t, 16, Q), F32), *([table] * 14),
            VMEM((GROUPS, Q, N), BF16), VMEM((GROUPS, Q, N), BF16), VMEM((Q * GROUPS, N), F32),
            turned, turned, states, quarters, wires, wires, quarters, eighth, eighth, quarters, states, quarters,
            VMEM((n_t, chunk, N), BF16), halves, halves, VMEM((GROUPS, ROWS, Q), F32), maps, maps,
            VMEM((2, 8, Q), F32),
            VMEM((n_t, 8, Q), F32), VMEM((dp_inner, 8, Q), F32), VMEM((dp_outer, 8, Q), F32),
            sems((2, n_t)), sems((2, n_t)), sems((2, 1)), sems((2, CHIPS)), sems((2, CHIPS, SUBS)), sems((2, SUBS)),
            sems((2, CHIPS, SUBS)), sems((2, CHIPS, SUBS)), sems((2, GROUPS)), sems((2, sums)),
        ],
        compiler_params=pltpu.CompilerParams(vmem_limit_bytes=LIMIT, collective_id=0, has_side_effects=True),
        name="scan_backward",
    )(
        step_raw, own, features, grad_out, input_map.reshape(Q * GROUPS, N), output_map.reshape(Q * GROUPS, N),
        saved_states.reshape(-1, chunk, N),
    )
    return (
        dx,
        draw,
        db.reshape(Q, GROUPS, N),
        dc.reshape(Q, GROUPS, N),
        total[:, 0],
        total[:, Q // 2],
    )


def solution(mesh):
    placed = (
        P(("dp", "tensor"), None),
        P(("dp", "tensor"), None),
        P(("dp", "tensor"), None, None),
        P(("dp", "tensor"), None, None),
        P("tensor"),
        P("tensor"),
        P("dp", None, "tensor", None, None),
        P(("dp", "tensor"), None),
    )
    return jax.shard_map(
        on_device,
        mesh=mesh,
        in_specs=placed,
        out_specs=(
            P(("dp", "tensor"), None),
            P(("dp", "tensor"), None),
            P(("dp", "tensor"), None, None),
            P(("dp", "tensor"), None, None),
            P("tensor"),
            P("tensor"),
        ),
        check_vma=False,
    )
```

time: 470 us -> 91.8 us (0.20)
  the two profiles are of different devices: /device:TPU:32 before, /device:TPU:1 now
where the time goes in v2:
time: 91.8 us; the launch traced here: 90 us
  Pallas kernels  81.7 us (89%)
  local copies, waits for them, and re-layouts  6.87 us (7%)
    pallas_call x1, Pallas kernels, on_device(): pl.pallas_call(functools.partial(kernel, dp_inner), out_shape=[jax.ShapeD...  81.7 us
    unnamed x10, local copies, waits for them, and re-layouts  4.72 us

profile of v2, /device:TPU:1, one launch (start us, length us, event | category | flops | bytes accessed | tf_op | source)
XLA Modules:
  0.0 90.0 jit_solution(14522119364344243178)
XLA Ops:
  0.6 0.7 pad_maximum_fusion
  1.4 0.7 broadcast_in_dim.2.own_ref
  2.1 81.7 %scan_backward.1 = (bf16[128,4096]{1,0:T(8,128)(2,1)}, f32[128,128]{1,0:T(8,128)}, bf16[1024,128]{1,0:T(8,128)(2,1)}, bf16[1024,128]{1,0:T(8,128)(2,1)}, f32[8,128]{1,0:T(8,128)}) custom-call(bf16[128,128]{1,0:T(8,128)(2,1)} %raw_ref.1, f32[16,128]{1,0:T(8,128)} %broadcast_in_dim.2.own_ref, bf16[128,4096]{1,0:T(8,128)(2,1)} %x_ref.1, ...), custom_call_target="tpu_custom_call" | custom-call | tf_op jit(solution)/shard_map/scan_backward/pallas_call | solution.py:494
  83.8 1.5 %slice_reduce_fusion = (f32[8]{0:T(128)}, f32[8]{0:T(128)}) fusion(f32[8,128]{1,0:T(8,128)} %get-tuple-element.15), kind=kLoop, calls=%fused_computation | loop fusion | bytes 128 | tf_op jit(solution)/shard_map/slice | solution.py:527
  85.3 0.0 copy-start.2
  85.3 0.0 copy-start.1
  85.3 2.3 %copy.18 = bf16[128,4096]{1,0:T(8,128)(2,1)} copy(bf16[128,4096]{1,0:T(8,128)(2,1)} %get-tuple-element.24) | data formatting | bytes 2097152
  87.6 0.0 copy-done.2
  87.6 0.6 copy.19
  88.3 0.0 copy-done.1
  88.3 0.0 copy-start
  88.3 0.7 copy.20
  89.0 0.3 copy-done
  89.3 0.7 copy.21
Async XLA Ops:
  85.3 2.3 %copy-start.2 = (f32[128,128]{1,0:T(8,128)S(1)}, f32[128,128]{1,0:T(8,128)}, u32[]{:S(2)}) copy-start(f32[128,128]{1,0:T(8,128)} %get-tuple-element.25) | copy-start | bytes 196612
  85.3 3.0 %copy-start.1 = (bf16[1024,128]{1,0:T(8,128)(2,1)S(1)}, bf16[1024,128]{1,0:T(8,128)(2,1)}, u32[]{:S(2)}) copy-start(bf16[1024,128]{1,0:T(8,128)(2,1)} %get-tuple-element.13) | copy-start | bytes 786436
  88.3 1.0 %copy-start = (bf16[1024,128]{1,0:T(8,128)(2,1)S(1)}, bf16[1024,128]{1,0:T(8,128)(2,1)}, u32[]{:S(2)}) copy-start(bf16[1024,128]{1,0:T(8,128)(2,1)} %get-tuple-element.14) | copy-start | bytes 786436

commit v3 on v2

v3 whole, which is shorter than its diff:
```python
import functools

import jax
import jax.numpy as jnp
from jax import lax
from jax.experimental import pallas as pl
from jax.experimental.pallas import tpu as pltpu
from jax.sharding import PartitionSpec as P

MESH = pl.DeviceIdType.MESH
F32 = jnp.float32
BF16 = jnp.bfloat16
VMEM = pltpu.VMEM
LIMIT = 56 * 1024 * 1024

Q = 128
N = 128
PW = 32
HEADS = 128
GROUPS = 8
PER = HEADS // GROUPS
ROWS = PER * PW


def split2(x):
    hi = x.astype(BF16)
    return hi, (x - hi.astype(F32)).astype(BF16)


def split3(x):
    hi = x.astype(BF16)
    rest = x - hi.astype(F32)
    mid = rest.astype(BF16)
    return hi, mid, (rest - mid.astype(F32)).astype(BF16)


def mm(a, b, ca=1, cb=0):
    return lax.dot_general(a, b, (((ca,), (cb,)), ((), ())), preferred_element_type=F32)


def lane_sums(x, ones):
    return mm(jnp.concatenate(split3(x), axis=1), jnp.concatenate([ones] * 3, axis=0))


def iota(dim):
    return lax.broadcasted_iota(jnp.int32, (Q, Q), dim)


def expand(x):
    return jnp.broadcast_to(x[:, None, :], (x.shape[0], PW, x.shape[1])).reshape(-1, x.shape[1])


def head_sums(x):
    return x.reshape(-1, PW, x.shape[1]).sum(axis=1)

CHIPS = 4
SUBS = 4
SUB = ROWS // SUBS
HEADS_SUB = PER // SUBS
WIRE = SUB + 8


def loop(lo, hi, body):
    def step(i, carry):
        body(i)
        return carry

    lax.fori_loop(lo, hi, step, 0)


def several(lo, hi, at_once, body):
    def step(k):
        for j in range(at_once):
            body(lo + at_once * k + j)

    loop(0, (hi - lo) // at_once, step)


def spans(i, size):
    return pl.ds(pl.multiple_of(i * size, size), size)


def kernel(
    dp_inner,
    dl_ref, sk_ref, raw_hbm, x_hbm, y_hbm, b_hbm, c_hbm, saved_hbm,
    dx_hbm, draw_hbm, db_hbm, dc_hbm, total_ref,
    raw_s, x_s, y_s, b_in, c_in, saved_s, own_s,
    gath, fsib, e4, f4, w4, k4, ends4, thr4,
    cum_s, v_s, u_s, r_s, z_s, s_s, sig_s, a_s, fall_s, draw_s, wide_f32, bm, cm, xt, yt,
    d_own, d_out, dsib, comp, cin, rout, yout, yin, rin, g_own, g_out, g_sib,
    esaved, est, mout, dxt, gb_s, dx_s, db_acc, dc_acc,
    part, from_t, from_i, from_o,
    load_sem, own_sem, saved_sem, f_sem, d_sem, in_sem, y_sem, ret_sem, g_sem, made_sem, sum_sem, store_sem,
):
    me = lax.axis_index("tensor")
    rep = lax.axis_index("dp")
    n_t, n_i, n_o = from_t.shape[0], from_i.shape[0], from_o.shape[0]
    core = lax.rem(me, 2)
    even = core == 0
    pair = me // 2
    x = lax.rem(pair, CHIPS)
    row = pair // CHIPS
    sib = me + 1 - 2 * core
    inner, outer = lax.rem(rep, dp_inner), rep // dp_inner
    last_pair = pair == n_t // 2 - 1

    def dev_t(j):
        return {"tensor": lax.rem(me + j, n_t)}

    def dev_i(j):
        return {"dp": outer * dp_inner + lax.rem(inner + j, n_i)}

    def dev_o(j):
        return {"dp": lax.rem(outer + j, n_o) * dp_inner + inner}

    def remote(src, dst, sems, i, j, dev):
        return pltpu.make_async_remote_copy(
            src_ref=src, dst_ref=dst, send_sem=sems.at[(0, *i)], recv_sem=sems.at[(1, *j)],
            device_id=dev, device_id_type=MESH,
        )

    loads = [
        pltpu.make_async_copy(src, dst, load_sem.at[i])
        for i, (src, dst) in enumerate(
            ((raw_hbm, raw_s), (saved_hbm, saved_s), (b_hbm, b_in), (c_hbm, c_in), (y_hbm, y_s), (x_hbm, x_s))
        )
    ]
    for load in loads:
        load.start()
    barrier = pltpu.get_barrier_semaphore()
    for n, dev in ((n_t, dev_t), (n_i, dev_i), (n_o, dev_o)):
        loop(1, n, lambda j: pl.semaphore_signal(barrier, inc=1, device_id=dev(j), device_id_type=MESH))
    for h in range(8):
        own_s[h : h + 1, :] = jnp.full((1, Q), dl_ref[h], F32)
        own_s[8 + h : 9 + h, :] = jnp.full((1, Q), sk_ref[h], F32)
    loads[0].wait()
    raw = raw_s[...].astype(F32).T
    small = jnp.exp(-jnp.abs(raw))
    s = jnp.maximum(raw, 0.0) + jnp.log1p(small)
    sig_s[...] = jnp.where(raw >= 0, 1.0, small) / (1.0 + small)
    s_s[...] = s
    loads[1].wait()
    pl.semaphore_wait(barrier, n_t - 1 + n_i - 1 + n_o - 1)

    def own_copy(j):
        return remote(own_s, gath.at[me], own_sem, (j,), (j,), dev_t(j))

    def saved_copy(k):
        return remote(saved_s.at[k - 1], esaved.at[me], saved_sem, (k,), (me,), {"tensor": 2 * k})

    def saved_arrival(t):
        return remote(saved_s.at[0], esaved.at[t], saved_sem, (0,), (t,), {"tensor": sib})

    def send_saved(k):
        @pl.when(me != 2 * k)
        def _():
            saved_copy(k).start()

        @pl.when(me == 2 * k)
        def _():
            esaved[me] = saved_s[k - 1]

    loop(1, n_t, lambda j: own_copy(j).start())
    loop(1, n_t // 2, send_saved)
    gath[me] = own_s[...]

    loads[2].wait()
    loads[3].wait()
    for src, dst in ((b_in, bm), (c_in, cm)):
        wide_f32[...] = src[...].astype(F32)
        for g in range(GROUPS):
            dst[g] = wide_f32[pl.ds(g, Q, stride=GROUPS), :].astype(BF16)
    loads[4].wait()
    loads[5].wait()

    def turn(g):
        for src, dst in ((y_s, yt), (x_s, xt)):
            dst[g] = src[:, spans(g, ROWS)].astype(F32).T.astype(BF16)

    loop(0, GROUPS, turn)

    loop(1, n_t, lambda j: own_copy(j).wait())
    a = jnp.exp(gath[:, 0:8, :].reshape(HEADS, Q))
    a_s[...] = a
    k4[...] = gath[:, 8:16, :].reshape(k4.shape)
    cum = lane_sums(-a * s, (iota(0) <= iota(1)).astype(F32).astype(BF16))
    last = jnp.broadcast_to(cum[:, Q - 1 : Q], (HEADS, Q))
    fall = jnp.exp(last)
    fall_s[...] = fall
    f4[...] = fall.reshape(f4.shape)
    f_copy = remote(f4, fsib, f_sem, (0,), (0,), {"tensor": sib})
    f_copy.start()
    e4[...] = jnp.exp(cum).reshape(e4.shape)

    def sub_rows(t):
        return spans(t, SUB)

    def d_copy(t):
        return remote(d_out.at[t], dsib.at[t], d_sem, (t,), (t,), {"tensor": sib})

    def d_of(g, t):
        hi, lo = split2(yt[g, sub_rows(t), :].astype(F32) * expand(e4[g, t]))
        m = cm[g]
        return mm(jnp.concatenate([hi, lo], axis=1), jnp.concatenate([m, m], axis=0))

    def made(t):
        for q in range(CHIPS):
            d_out[t, q] = d_of(2 * q + 1 - core, t)
        d_copy(t).start()
        for q in range(CHIPS):
            d_own[t, q] = d_of(2 * q + core, t)

    def in_copy(t, q):
        return remote(
            comp.at[t, q], cin.at[t, x], in_sem, (t, q), (t, x), {"tensor": row * 2 * CHIPS + 2 * q + core}
        )

    def in_arrival(t, j):
        return remote(comp.at[t, j], cin.at[t, j], in_sem, (t, j), (t, j), {"tensor": sib})

    def fold(t):
        d_copy(t).wait_recv()

        def quarter(q):
            g = 2 * q + core
            f_here, f_there = f4[g, t], fsib[g, t]
            f_even, f_odd = jnp.where(even, f_here, f_there), jnp.where(even, f_there, f_here)
            d_here, d_there = d_own[t, q], dsib[t, q]
            d_even, d_odd = jnp.where(even, d_here, d_there), jnp.where(even, d_there, d_here)
            comp[t, q, 0:SUB, :] = d_even + expand(f_even) * d_odd
            f_both = f_even * f_odd
            comp[t, q, SUB:WIRE, :] = jnp.concatenate([f_both, f_both], axis=0)

            @pl.when(q != x)
            def _():
                in_copy(t, q).start()

            @pl.when(q == x)
            def _():
                cin[t, x] = comp[t, q]

        loop(0, CHIPS, quarter)

    made(0)
    made(1)
    f_copy.wait()
    fold(0)
    made(2)
    fold(1)
    made(3)
    fold(2)
    fold(3)

    cum_s[...] = cum.reshape(cum_s.shape)
    v_s[...] = (cum - jnp.log(s_s[...])).reshape(v_s.shape)
    w4[...] = (jnp.exp(last - cum) * s_s[...]).reshape(w4.shape)

    @pl.when(last_pair)
    def _():
        rin[...] = jnp.zeros(rin.shape, F32)

    inside = iota(0) >= iota(1)
    head_of = iota(0) // PW
    lane = lax.broadcasted_iota(jnp.int32, (PER, Q), 1)

    def local(g):
        b, c = bm[g], cm[g]
        m = mm(c, b, 1, 1)
        v = v_s[g]
        cum_n = cum_s[g].T
        dm = jnp.zeros((Q, Q), F32)
        for q in range(PER // 4):
            x4 = xt[g, q * Q : (q + 1) * Q, :].astype(F32)
            wide = jnp.concatenate([jnp.where(head_of == h, x4, 0.0).astype(BF16) for h in range(4)], axis=1)
            y4 = y_s[:, pl.ds(pl.multiple_of(g * ROWS + q * Q, Q), Q)]
            ds4 = mm(y4, wide)
            for h in range(4):
                hh = 4 * q + h
                mine = slice(hh * PW, (hh + 1) * PW)
                xh, yh = xt[g, mine, :], yt[g, mine, :]
                spread = cum_n[:, hh : hh + 1] - v[hh : hh + 1, :]
                decay = jnp.exp(jnp.where(inside, spread, -1e30))
                scores = m * decay
                dm = dm + ds4[:, h * Q : (h + 1) * Q] * decay
                both = jnp.concatenate(split2(scores), axis=0)
                dxw = mm(jnp.concatenate([yh, yh], axis=1), both)
                within = mm(xh, both, 1, 1)
                within = within[:, :Q] + within[:, Q:]
                dxt[g, mine, :] = dxw
                u_s[g, hh : hh + 1, :] = jnp.sum(xh.astype(F32) * dxw, axis=0, keepdims=True)
                r_s[g, hh : hh + 1, :] = jnp.sum(yh.astype(F32) * within, axis=0, keepdims=True)
        dm_hi, dm_lo = split2(dm)
        dc_acc[g] = mm(jnp.concatenate([dm_hi, dm_lo], axis=1), jnp.concatenate([b, b], axis=0))
        db_acc[g] = mm(jnp.concatenate([dm_hi, dm_lo], axis=0), jnp.concatenate([c, c], axis=0), 0, 0)
        z_s[g] = jnp.broadcast_to(
            jnp.sum(head_sums(yt[g].astype(F32) * xt[g].astype(F32)), axis=1, keepdims=True), (PER, Q)
        )

    def y_copy(t):
        return remote(yout.at[t], yin.at[t], y_sem, (t,), (t,), {"tensor": me - row * 2 * CHIPS})

    def ret_copy(t, j):
        return remote(
            rout.at[t, j], rin.at[t, x], ret_sem, (t, j), (t, x), {"tensor": row * 2 * CHIPS + 2 * j + core}
        )

    def ret_arrival(t, q):
        return remote(rout.at[t, q], rin.at[t, q], ret_sem, (t, q), (t, q), {"tensor": sib})

    def hand_back(t, j):
        @pl.when(j != x)
        def _():
            ret_copy(t, j).start()

        @pl.when(j == x)
        def _():
            rin[t, x] = rout[t, j]

    def factor(t, j):
        return cin[t, j, SUB : SUB + HEADS_SUB, :]

    def scan(t):
        for j in range(CHIPS):

            @pl.when(j != x)
            def _():
                in_arrival(t, j).wait_recv()

        state = cin[t, CHIPS - 1, 0:SUB, :]
        for j in range(CHIPS - 2, -1, -1):
            rout[t, j] = state
            state = cin[t, j, 0:SUB, :] + expand(factor(t, j)) * state

        @pl.when(row == 1)
        def _():
            yout[t] = state
            y_copy(t).start()
            loop(0, CHIPS - 1, lambda j: hand_back(t, j))

    def row_back(t):
        @pl.when(row == 0)
        def _():
            y_copy(t).wait_recv()
            coming = yin[t]
            rout[t, CHIPS - 1] = coming
            through = factor(t, CHIPS - 1)
            for j in range(CHIPS - 2, -1, -1):
                rout[t, j] = rout[t, j] + expand(through) * coming
                if j > 0:
                    through = through * factor(t, j)
            loop(0, CHIPS, lambda j: hand_back(t, j))

    def made_copy(g):
        return remote(mout.at[g], est.at[g], made_sem, (g,), (g,), {"tensor": sib})

    def whole_group(x4):
        return jnp.concatenate([expand(x4[t]) for t in range(SUBS)], axis=0)

    def even_states(g):
        @pl.when(even)
        def _():
            @pl.when(pair > 0)
            def _():
                for i in range(2):
                    t = 2 * g + i

                    @pl.when(t != me)
                    def _():
                        saved_arrival(t).wait_recv()

                    est[g, i] = esaved[t].astype(F32)

            @pl.when(pair == 0)
            def _():
                est[g] = jnp.zeros(est.shape[1:], F32)

            hi, lo = split2(xt[g].astype(F32) * whole_group(w4[g]))
            m = bm[g]
            added = mm(jnp.concatenate([hi, lo], axis=1), jnp.concatenate([m, m], axis=0))
            mout[g] = (whole_group(f4[g]) * est[g].reshape(ROWS, N) + added).reshape(mout.shape[1:])
            made_copy(g).start()

    def arrived_states(g):
        @pl.when(core == 1)
        def _():
            made_copy(g).wait_recv()

    def from_states(g):
        e_state = est[g].reshape(ROWS, N)
        e_hi, e_lo = split2(e_state)
        c = cm[g]
        ey = whole_group(e4[g]) * yt[g].astype(F32)
        ey_hi, ey_lo = split2(ey)
        ec = mm(jnp.concatenate([e_hi, e_lo], axis=1), jnp.concatenate([c, c], axis=1), 1, 1)
        r_s[g] = r_s[g] + head_sums(ey * ec)
        dc_acc[g] = dc_acc[g] + mm(ey_hi, e_hi, 0, 0) + mm(ey_hi, e_lo, 0, 0) + mm(ey_lo, e_hi, 0, 0)

    def g_copy(t):
        return remote(g_out.at[t], g_sib.at[t], g_sem, (t,), (t,), {"tensor": sib})

    def coming_back(t):
        def quarter(q):
            g = 2 * q + core

            @pl.when(jnp.logical_and(q != x, jnp.logical_not(last_pair)))
            def _():
                ret_arrival(t, q).wait_recv()

            coming = rin[t, q]
            f_odd = jnp.where(even, fsib[g, t], f4[g, t])
            d_odd = jnp.where(even, dsib[t, q], d_own[t, q])
            to_even = d_odd + expand(f_odd) * coming
            g_own[t, q] = jnp.where(even, to_even, coming)
            g_out[t, q] = jnp.where(even, coming, to_even)

        loop(0, CHIPS, quarter)
        g_copy(t).start()

    def step_part(g, t, state):
        b = bm[g]
        gb = mm(jnp.concatenate(split2(state), axis=1), jnp.concatenate([b, b], axis=1), 1, 1)
        gb_s[g, sub_rows(t), :] = gb
        wx = expand(w4[g, t]) * xt[g, sub_rows(t), :].astype(F32)
        ends4[g, t] = head_sums(wx * gb)
        e_state = est[g, t // 2, spans(t % 2, SUB), :]
        thr4[g, t] = jnp.broadcast_to(
            jnp.sum(head_sums(e_state * state), axis=1, keepdims=True), (HEADS_SUB, Q)
        )

    def map_part(g, t, state):
        xf, yf = xt[g, sub_rows(t), :].astype(F32), yt[g, sub_rows(t), :].astype(F32)
        ex_w = expand(w4[g, t])
        g_hi, g_lo = split2(state)
        wx_hi, wx_lo = split2(ex_w * xf)
        db_acc[g] = db_acc[g] + mm(wx_hi, g_hi, 0, 0) + mm(wx_hi, g_lo, 0, 0) + mm(wx_lo, g_hi, 0, 0)
        dx = dxt[g, sub_rows(t), :] + ex_w * gb_s[g, sub_rows(t), :] + expand(k4[g, t]) * yf
        dx_s[:, pl.ds(pl.multiple_of(g * ROWS + t * SUB, SUB), SUB)] = dx.T.astype(BF16)

    def steps(t):
        for q in range(CHIPS):
            step_part(2 * q + core, t, g_own[t, q])
        g_copy(t).wait_recv()
        for q in range(CHIPS):
            step_part(2 * q + 1 - core, t, g_sib[t, q])

    def maps(t):
        def quarter(q):
            map_part(2 * q + core, t, g_own[t, q])
            map_part(2 * q + 1 - core, t, g_sib[t, q])

        several(0, CHIPS, 2, quarter)

    loop(0, 3, local)
    scan(0)
    loop(3, 5, local)
    scan(1)
    loop(5, 7, local)
    scan(2)
    loop(7, 8, local)
    loop(0, 4, even_states)
    scan(3)
    loop(4, 8, even_states)
    row_back(0)
    loop(0, 4, arrived_states)
    several(0, 4, 2, from_states)
    row_back(1)
    loop(4, 8, arrived_states)
    several(4, 8, 2, from_states)
    coming_back(0)
    row_back(2)
    steps(0)
    coming_back(1)
    row_back(3)
    maps(0)
    coming_back(2)
    steps(1)
    maps(1)
    coming_back(3)
    steps(2)
    maps(2)
    steps(3)

    lanes = lax.broadcasted_iota(jnp.int32, (HEADS, Q), 1)
    ends = ends4[...].reshape(HEADS, Q)
    u = u_s[...].reshape(HEADS, Q)
    at_end = thr4[...].reshape(HEADS, Q) * fall_s[...] + jnp.sum(ends, axis=1, keepdims=True)
    dcum = r_s[...].reshape(HEADS, Q) - u - ends + jnp.where(lanes == Q - 1, at_end, 0.0)
    drate = lane_sums(dcum, (iota(0) >= iota(1)).astype(F32).astype(BF16))
    ra = a_s[...]
    rs = s_s[...]
    decay_part = jnp.sum(drate * (-ra * rs), axis=1, keepdims=True)
    z_s[...] = jnp.where(lanes < Q // 2, decay_part, z_s[...].reshape(HEADS, Q)).reshape(z_s.shape)

    def exchange(n, dev, at, source, landing, base, beside):
        def copy(j):
            return remote(source(j), landing.at[at], sum_sem, (base + j,), (base + j,), dev(j))

        loop(1, n, lambda j: copy(j).start())
        landing[at] = source(0)[...]
        beside()
        loop(1, n, lambda j: copy(j).wait())
        return jnp.sum(landing[...], axis=0)

    def z_part(j):
        t = lax.rem(me + j, n_t)
        return z_s.at[t // 2, spans(lax.rem(t, 2), 8), :]

    stores = [
        pltpu.make_async_copy(src, dst, store_sem.at[i])
        for i, (src, dst) in enumerate(((dx_s, dx_hbm), (draw_s, draw_hbm), (b_in, db_hbm), (c_in, dc_hbm)))
    ]

    def write_maps(acc, out):
        for g in range(GROUPS):
            wide_f32[pl.ds(g, Q, stride=GROUPS), :] = acc[g]
        out[...] = wide_f32[...].astype(BF16)

    def beside_t():
        maps(3)
        stores[0].start()

    def beside_i():
        draw_s[...] = ((-ra * drate + (u + ends) / rs) * sig_s[...]).T
        stores[1].start()
        write_maps(db_acc, b_in)
        stores[2].start()

    def beside_o():
        write_maps(dc_acc, c_in)
        stores[3].start()

    part[0] = exchange(n_t, dev_t, me, z_part, from_t, 0, beside_t)
    part[1] = exchange(n_i, dev_i, inner, lambda j: part.at[0], from_i, n_t, beside_i)
    total_ref[...] = exchange(n_o, dev_o, outer, lambda j: part.at[1], from_o, n_t + n_i, beside_o)

    for store in stores:
        store.wait()

    def sent_saved(k):
        @pl.when(me != 2 * k)
        def _():
            saved_copy(k).wait_send()

    loop(1, n_t // 2, sent_saved)

    def sent(t):
        d_copy(t).wait_send()
        g_copy(t).wait_send()

        @pl.when(row == 1)
        def _():
            y_copy(t).wait_send()

        def quarter(q):
            @pl.when(q != x)
            def _():
                in_copy(t, q).wait_send()

                @pl.when(jnp.logical_or(row == 0, q < CHIPS - 1))
                def _():
                    ret_copy(t, q).wait_send()

        loop(0, CHIPS, quarter)

    loop(0, SUBS, sent)

    @pl.when(even)
    def _():
        loop(0, GROUPS, lambda g: made_copy(g).wait_send())


def finish_kernel(dx_in, draw_in, db_in, dc_in, total_ref, dx, draw, db, dc, decay, skip):
    for src, dst in ((dx_in, dx), (draw_in, draw), (db_in, db), (dc_in, dc)):
        dst[...] = src[...]
    turned = total_ref[...].T
    decay[...] = turned[0, :]
    skip[...] = turned[Q // 2, :]


def on_device(features, step_raw, input_map, output_map, decay_log, skip_gain, saved_states, grad_out):
    n_t = lax.axis_size("tensor")
    n_dp = lax.axis_size("dp")
    whole = pl.BlockSpec(memory_space=VMEM)
    away = pl.BlockSpec(memory_space=pl.ANY)
    scalars = pl.BlockSpec(memory_space=pltpu.SMEM)
    dp_inner = 8 if n_dp % 8 == 0 else n_dp
    dp_outer = n_dp // dp_inner
    sums = n_t + dp_inner + dp_outer
    table = VMEM((HEADS, Q), F32)
    by_group = VMEM((GROUPS, PER, Q), F32)
    by_sub = VMEM((GROUPS, SUBS, HEADS_SUB, Q), F32)
    turned = VMEM((GROUPS, ROWS, Q), BF16)
    quarters = VMEM((SUBS, CHIPS, SUB, N), F32)
    wires = VMEM((SUBS, CHIPS, WIRE, N), F32)
    eighth = VMEM((SUBS, SUB, N), F32)
    chunk = HEADS * PW // n_t
    halves = VMEM((GROUPS, 2, chunk, N), F32)
    maps = VMEM((GROUPS, Q, N), F32)
    by_rows = VMEM((GROUPS, ROWS, Q), F32)
    flat_map = VMEM((Q * GROUPS, N), BF16)
    wide = VMEM((Q, HEADS * PW), BF16)
    sems = pltpu.SemaphoreType.DMA
    shapes = [
        jax.ShapeDtypeStruct((Q, HEADS * PW), BF16),
        jax.ShapeDtypeStruct((Q, HEADS), F32),
        jax.ShapeDtypeStruct((Q * GROUPS, N), BF16),
        jax.ShapeDtypeStruct((Q * GROUPS, N), BF16),
    ]
    results = pl.pallas_call(
        functools.partial(kernel, dp_inner),
        out_shape=[*shapes, jax.ShapeDtypeStruct((8, Q), F32)],
        in_specs=[scalars] * 2 + [away] * 6,
        out_specs=[away] * 4 + [whole],
        scratch_shapes=[
            VMEM((Q, HEADS), BF16), wide, wide, flat_map, flat_map, VMEM((n_t // 2 - 1, chunk, N), BF16),
            VMEM((16, Q), F32),
            VMEM((n_t, 16, Q), F32), *([by_sub] * 7),
            *([by_group] * 5), *([table] * 5),
            VMEM((Q * GROUPS, N), F32), VMEM((GROUPS, Q, N), BF16), VMEM((GROUPS, Q, N), BF16), turned, turned,
            *([quarters] * 3), wires, wires, quarters, eighth, eighth, *([quarters] * 4),
            VMEM((n_t, chunk, N), BF16), halves, halves, by_rows, by_rows, wide, maps, maps,
            VMEM((2, 8, Q), F32),
            VMEM((n_t, 8, Q), F32), VMEM((dp_inner, 8, Q), F32), VMEM((dp_outer, 8, Q), F32),
            sems((6,)), sems((2, n_t)), sems((2, n_t)), sems((2, 1)), sems((2, SUBS)), sems((2, SUBS, CHIPS)),
            sems((2, SUBS)), sems((2, SUBS, CHIPS)), sems((2, SUBS)), sems((2, GROUPS)), sems((2, sums)), sems((4,)),
        ],
        compiler_params=pltpu.CompilerParams(vmem_limit_bytes=LIMIT, collective_id=0, has_side_effects=True),
        name="scan_backward",
    )(
        decay_log, skip_gain, step_raw, features, grad_out, input_map.reshape(Q * GROUPS, N),
        output_map.reshape(Q * GROUPS, N), saved_states.reshape(-1, chunk, N),
    )
    vector = jax.ShapeDtypeStruct((8,), F32)
    dx, draw, db, dc, decay, skip = pl.pallas_call(
        finish_kernel,
        out_shape=[*shapes, vector, vector],
        in_specs=[whole] * 5,
        out_specs=[whole] * 6,
        compiler_params=pltpu.CompilerParams(vmem_limit_bytes=LIMIT),
        name="finish",
    )(*results)
    return (dx, draw, db.reshape(Q, GROUPS, N), dc.reshape(Q, GROUPS, N), decay, skip)


def solution(mesh):
    placed = (
        P(("dp", "tensor"), None),
        P(("dp", "tensor"), None),
        P(("dp", "tensor"), None, None),
        P(("dp", "tensor"), None, None),
        P("tensor"),
        P("tensor"),
        P("dp", None, "tensor", None, None),
        P(("dp", "tensor"), None),
    )
    return jax.shard_map(
        on_device,
        mesh=mesh,
        in_specs=placed,
        out_specs=(
            P(("dp", "tensor"), None),
            P(("dp", "tensor"), None),
            P(("dp", "tensor"), None, None),
            P(("dp", "tensor"), None, None),
            P("tensor"),
            P("tensor"),
        ),
        check_vma=False,
    )
```

time: 91.8 us -> 77.6 us (0.85)
  local copies, waits for them, and re-layouts: 6.87 us -> 0 us
  Pallas kernels: 81.7 us -> 75.9 us
    pallas_call x1 -> x2, Pallas kernels: 81.7 us -> 75.9 us  [the longest x1 73.3 us: on_device(): pl.pallas_call(functools.partial(kernel, dp_inner), out_shape=[*shapes, j...]
    unnamed x10 -> x0, local copies, waits for them, and re-layouts: 4.72 us -> none
    slice x1 -> x0, local copies, waits for them, and re-layouts: 1.48 us -> none  [on_device(): total[:, Q // 2]]
where the time goes in v3:
time: 77.6 us; the launch traced here: 76.5 us
  Pallas kernels  75.9 us (98%)
    pallas_call x1, Pallas kernels, on_device(): pl.pallas_call(functools.partial(kernel, dp_inner), out_shape=[*shapes, j...  73.3 us
    pallas_call x1, Pallas kernels, on_device(): pl.pallas_call(finish_kernel, out_shape=[*shapes, vector, vector], in_spe...  2.56 us

profile of v3, /device:TPU:1, one launch (start us, length us, event | category | flops | bytes accessed | tf_op | source)
XLA Modules:
  0.0 76.5 jit_solution(7921321061496468563)
XLA Ops:
  0.6 73.3 %scan_backward.1 = (bf16[128,4096]{1,0:T(8,128)(2,1)}, f32[128,128]{1,0:T(8,128)}, bf16[1024,128]{1,0:T(8,128)(2,1)}, bf16[1024,128]{1,0:T(8,128)(2,1)}, f32[8,128]{1,0:T(8,128)}) custom-call(f32[8]{0:T(128)} %dl_ref.1, f32[8]{0:T(128)} %sk_ref.1, bf16[128,128]{1,0:T(8,128)(2,1)} %raw_hbm.1, bf16[128,4096]{1,0:T(8,128)(2,1)} %x_hbm.1, ...), custom_call_target="tpu_custom_call" | custom-call | tf_op jit(solution)/shard_map/scan_backward/pallas_call | solution.py:609
  74.0 2.6 %finish.1 = (bf16[128,4096]{1,0:T(8,128)(2,1)}, f32[128,128]{1,0:T(8,128)}, bf16[1024,128]{1,0:T(8,128)(2,1)}, bf16[1024,128]{1,0:T(8,128)(2,1)}, f32[8]{0:T(128)}, /*index=5*/f32[8]{0:T(128)}) custom-call(bf16[128,4096]{1,0:T(8,128)(2,1)} %get-tuple-element.17.dx_in, f32[128,128]{1,0:T(8,128)} %get-tuple-element.18.draw_in, ...), custom_call_target="tpu_custom_call" | custom-call | tf_op jit(solution)/shard_map/finish/pallas_call | solution.py:634

commit v4 on v3

--- a/solution.py
+++ b/solution.py
@@ -89,29 +89,39 @@
     cum_s, v_s, u_s, r_s, z_s, s_s, sig_s, a_s, fall_s, draw_s, wide_f32, bm, cm, xt, yt,
     d_own, d_out, dsib, comp, cin, rout, yout, yin, rin, g_own, g_out, g_sib,
     esaved, est, mout, dxt, gb_s, dx_s, db_acc, dc_acc,
-    part, from_t, from_i, from_o,
+    z_out, part_x, part_y, from_x, from_y, from_z,
     load_sem, own_sem, saved_sem, f_sem, d_sem, in_sem, y_sem, ret_sem, g_sem, made_sem, sum_sem, store_sem,
 ):
     me = lax.axis_index("tensor")
     rep = lax.axis_index("dp")
-    n_t, n_i, n_o = from_t.shape[0], from_i.shape[0], from_o.shape[0]
+    n_t = gath.shape[0]
+    n_x, n_y, n_z = from_x.shape[0], from_y.shape[0], from_z.shape[0]
     core = lax.rem(me, 2)
     even = core == 0
     pair = me // 2
     x = lax.rem(pair, CHIPS)
     row = pair // CHIPS
     sib = me + 1 - 2 * core
-    inner, outer = lax.rem(rep, dp_inner), rep // dp_inner
+    place = lax.rem(me, n_x)
+    z_at, y_low = lax.rem(rep, dp_inner), rep // dp_inner
+    y_lows = n_y // (n_t // n_x)
+    y_at = row * y_lows + y_low
     last_pair = pair == n_t // 2 - 1
 
     def dev_t(j):
         return {"tensor": lax.rem(me + j, n_t)}
 
-    def dev_i(j):
-        return {"dp": outer * dp_inner + lax.rem(inner + j, n_i)}
-
-    def dev_o(j):
-        return {"dp": lax.rem(outer + j, n_o) * dp_inner + inner}
+    def dev_x(j):
+        return {"tensor": row * n_x + lax.rem(place + j, n_x)}
+
+    def y_of(j):
+        return lax.rem(y_at + j, n_y)
+
+    def dev_y(j):
+        return {"tensor": y_of(j) // y_lows * n_x + place, "dp": lax.rem(y_of(j), y_lows) * dp_inner + z_at}
+
+    def dev_z(j):
+        return {"dp": y_low * dp_inner + lax.rem(z_at + j, n_z)}
 
     def remote(src, dst, sems, i, j, dev):
         return pltpu.make_async_remote_copy(
@@ -128,11 +138,24 @@
     for load in loads:
         load.start()
     barrier = pltpu.get_barrier_semaphore()
-    for n, dev in ((n_t, dev_t), (n_i, dev_i), (n_o, dev_o)):
-        loop(1, n, lambda j: pl.semaphore_signal(barrier, inc=1, device_id=dev(j), device_id_type=MESH))
+
+    def greet(dev):
+        pl.semaphore_signal(barrier, inc=1, device_id=dev, device_id_type=MESH)
+
+    def greet_y(j):
+        @pl.when(lax.rem(y_of(j), y_lows) != y_low)
+        def _():
+            greet(dev_y(j))
+
+    loop(1, n_t, lambda j: greet(dev_t(j)))
+    loop(1, n_y, greet_y)
+    loop(1, n_z, lambda j: greet(dev_z(j)))
+    spot = lax.broadcasted_iota(jnp.int32, (1, Q), 1)
+    params = jnp.zeros((1, Q), F32)
     for h in range(8):
-        own_s[h : h + 1, :] = jnp.full((1, Q), dl_ref[h], F32)
-        own_s[8 + h : 9 + h, :] = jnp.full((1, Q), sk_ref[h], F32)
+        params = jnp.where(spot == h, dl_ref[h], params)
+        params = jnp.where(spot == 8 + h, sk_ref[h], params)
+    own_s[...] = params
     loads[0].wait()
     raw = raw_s[...].astype(F32).T
     small = jnp.exp(-jnp.abs(raw))
@@ -140,10 +163,10 @@
     sig_s[...] = jnp.where(raw >= 0, 1.0, small) / (1.0 + small)
     s_s[...] = s
     loads[1].wait()
-    pl.semaphore_wait(barrier, n_t - 1 + n_i - 1 + n_o - 1)
+    pl.semaphore_wait(barrier, n_t - 1 + n_y - n_y // y_lows + n_z - 1)
 
     def own_copy(j):
-        return remote(own_s, gath.at[me], own_sem, (j,), (j,), dev_t(j))
+        return remote(own_s, gath.at[me], own_sem, (j,), (j,), dev_t(lax.rem(j + 3, n_t - 1) + 1))
 
     def saved_copy(k):
         return remote(saved_s.at[k - 1], esaved.at[me], saved_sem, (k,), (me,), {"tensor": 2 * k})
@@ -180,9 +203,13 @@
     loop(0, GROUPS, turn)
 
     loop(1, n_t, lambda j: own_copy(j).wait())
-    a = jnp.exp(gath[:, 0:8, :].reshape(HEADS, Q))
+    params = gath[...].reshape(n_t, Q)
+    for h in range(8):
+        a_s[pl.ds(h, n_t, stride=8), :] = jnp.broadcast_to(params[:, h : h + 1], (n_t, Q))
+        draw_s[pl.ds(h, n_t, stride=8), :] = jnp.broadcast_to(params[:, 8 + h : 9 + h], (n_t, Q))
+    a = jnp.exp(a_s[...])
     a_s[...] = a
-    k4[...] = gath[:, 8:16, :].reshape(k4.shape)
+    k4[...] = draw_s[...].reshape(k4.shape)
     cum = lane_sums(-a * s, (iota(0) <= iota(1)).astype(F32).astype(BF16))
     last = jnp.broadcast_to(cum[:, Q - 1 : Q], (HEADS, Q))
     fall = jnp.exp(last)
@@ -457,20 +484,17 @@
     loop(5, 7, local)
     scan(2)
     loop(7, 8, local)
-    loop(0, 4, even_states)
     scan(3)
-    loop(4, 8, even_states)
     row_back(0)
-    loop(0, 4, arrived_states)
-    several(0, 4, 2, from_states)
     row_back(1)
-    loop(4, 8, arrived_states)
-    several(4, 8, 2, from_states)
+    loop(0, GROUPS, even_states)
+    row_back(2)
+    row_back(3)
     coming_back(0)
-    row_back(2)
+    loop(0, GROUPS, arrived_states)
+    several(0, GROUPS, 2, from_states)
+    coming_back(1)
     steps(0)
-    coming_back(1)
-    row_back(3)
     maps(0)
     coming_back(2)
     steps(1)
@@ -489,21 +513,18 @@
     ra = a_s[...]
     rs = s_s[...]
     decay_part = jnp.sum(drate * (-ra * rs), axis=1, keepdims=True)
-    z_s[...] = jnp.where(lanes < Q // 2, decay_part, z_s[...].reshape(HEADS, Q)).reshape(z_s.shape)
+    turned = jnp.where(lanes < Q // 2, decay_part, z_s[...].reshape(HEADS, Q)).T
+    z_out[...] = jnp.concatenate([turned[0:1], turned[Q // 2 : Q // 2 + 1]], axis=0)
 
     def exchange(n, dev, at, source, landing, base, beside):
         def copy(j):
-            return remote(source(j), landing.at[at], sum_sem, (base + j,), (base + j,), dev(j))
+            return remote(source, landing.at[at], sum_sem, (base + j,), (base + j,), dev(j))
 
         loop(1, n, lambda j: copy(j).start())
-        landing[at] = source(0)[...]
+        landing[at] = source[...]
         beside()
         loop(1, n, lambda j: copy(j).wait())
         return jnp.sum(landing[...], axis=0)
-
-    def z_part(j):
-        t = lax.rem(me + j, n_t)
-        return z_s.at[t // 2, spans(lax.rem(t, 2), 8), :]
 
     stores = [
         pltpu.make_async_copy(src, dst, store_sem.at[i])
@@ -515,23 +536,25 @@
             wide_f32[pl.ds(g, Q, stride=GROUPS), :] = acc[g]
         out[...] = wide_f32[...].astype(BF16)
 
-    def beside_t():
+    def beside_x():
         maps(3)
         stores[0].start()
 
-    def beside_i():
+    def beside_y():
         draw_s[...] = ((-ra * drate + (u + ends) / rs) * sig_s[...]).T
         stores[1].start()
         write_maps(db_acc, b_in)
         stores[2].start()
 
-    def beside_o():
+    def beside_z():
         write_maps(dc_acc, c_in)
         stores[3].start()
 
-    part[0] = exchange(n_t, dev_t, me, z_part, from_t, 0, beside_t)
-    part[1] = exchange(n_i, dev_i, inner, lambda j: part.at[0], from_i, n_t, beside_i)
-    total_ref[...] = exchange(n_o, dev_o, outer, lambda j: part.at[1], from_o, n_t + n_i, beside_o)
+    part_x[...] = exchange(n_x, dev_x, place, z_out, from_x, 0, beside_x)
+    part_y[...] = exchange(n_y, dev_y, y_at, part_x, from_y, n_x, beside_y)
+    total = exchange(n_z, dev_z, z_at, part_y, from_z, n_x + n_y, beside_z)
+    mine = (iota(0) == 8 * me + iota(1)).astype(F32).astype(BF16)
+    total_ref[...] = lane_sums(jnp.concatenate([total] * 4, axis=0), mine)
 
     for store in stores:
         store.wait()
@@ -572,9 +595,8 @@
 def finish_kernel(dx_in, draw_in, db_in, dc_in, total_ref, dx, draw, db, dc, decay, skip):
     for src, dst in ((dx_in, dx), (draw_in, draw), (db_in, db), (dc_in, dc)):
         dst[...] = src[...]
-    turned = total_ref[...].T
-    decay[...] = turned[0, :]
-    skip[...] = turned[Q // 2, :]
+    decay[...] = total_ref[0, 0:8]
+    skip[...] = total_ref[1, 0:8]
 
 
 def on_device(features, step_raw, input_map, output_map, decay_log, skip_gain, saved_states, grad_out):
@@ -583,9 +605,10 @@
     whole = pl.BlockSpec(memory_space=VMEM)
     away = pl.BlockSpec(memory_space=pl.ANY)
     scalars = pl.BlockSpec(memory_space=pltpu.SMEM)
-    dp_inner = 8 if n_dp % 8 == 0 else n_dp
-    dp_outer = n_dp // dp_inner
-    sums = n_t + dp_inner + dp_outer
+    n_x = 2 * CHIPS
+    n_z = 8 if n_dp % 8 == 0 else 1
+    n_y = n_dp // n_z * (n_t // n_x)
+    sums = n_x + n_y + n_z
     table = VMEM((HEADS, Q), F32)
     by_group = VMEM((GROUPS, PER, Q), F32)
     by_sub = VMEM((GROUPS, SUBS, HEADS_SUB, Q), F32)
@@ -607,20 +630,20 @@
         jax.ShapeDtypeStruct((Q * GROUPS, N), BF16),
     ]
     results = pl.pallas_call(
-        functools.partial(kernel, dp_inner),
+        functools.partial(kernel, n_z),
         out_shape=[*shapes, jax.ShapeDtypeStruct((8, Q), F32)],
         in_specs=[scalars] * 2 + [away] * 6,
         out_specs=[away] * 4 + [whole],
         scratch_shapes=[
             VMEM((Q, HEADS), BF16), wide, wide, flat_map, flat_map, VMEM((n_t // 2 - 1, chunk, N), BF16),
-            VMEM((16, Q), F32),
-            VMEM((n_t, 16, Q), F32), *([by_sub] * 7),
+            VMEM((1, Q), F32),
+            VMEM((n_t, 1, Q), F32), *([by_sub] * 7),
             *([by_group] * 5), *([table] * 5),
             VMEM((Q * GROUPS, N), F32), VMEM((GROUPS, Q, N), BF16), VMEM((GROUPS, Q, N), BF16), turned, turned,
             *([quarters] * 3), wires, wires, quarters, eighth, eighth, *([quarters] * 4),
             VMEM((n_t, chunk, N), BF16), halves, halves, by_rows, by_rows, wide, maps, maps,
-            VMEM((2, 8, Q), F32),
-            VMEM((n_t, 8, Q), F32), VMEM((dp_inner, 8, Q), F32), VMEM((dp_outer, 8, Q), F32),
+            VMEM((2, Q), F32), VMEM((2, Q), F32), VMEM((2, Q), F32),
+            VMEM((n_x, 2, Q), F32), VMEM((n_y, 2, Q), F32), VMEM((n_z, 2, Q), F32),
             sems((6,)), sems((2, n_t)), sems((2, n_t)), sems((2, 1)), sems((2, SUBS)), sems((2, SUBS, CHIPS)),
             sems((2, SUBS)), sems((2, SUBS, CHIPS)), sems((2, SUBS)), sems((2, GROUPS)), sems((2, sums)), sems((4,)),
         ],
@@ -631,11 +654,13 @@
         output_map.reshape(Q * GROUPS, N), saved_states.reshape(-1, chunk, N),
     )
     vector = jax.ShapeDtypeStruct((8,), F32)
+    halves_of = [pl.BlockSpec((shape.shape[0] // 2, shape.shape[1]), lambda i: (i, 0)) for shape in shapes]
     dx, draw, db, dc, decay, skip = pl.pallas_call(
         finish_kernel,
         out_shape=[*shapes, vector, vector],
-        in_specs=[whole] * 5,
-        out_specs=[whole] * 6,
+        grid=(2,),
+        in_specs=[*halves_of, pl.BlockSpec((8, Q), lambda i: (0, 0))],
+        out_specs=[*halves_of, *([pl.BlockSpec((8,), lambda i: (0,))] * 2)],
         compiler_params=pltpu.CompilerParams(vmem_limit_bytes=LIMIT),
         name="finish",
     )(*results)

time: 77.6 us -> 73.4 us (0.946); the launches traced: 76.5 us -> 73.2 us
  Pallas kernels: 75.9 us -> 72.6 us
    pallas_call x2, Pallas kernels: 75.9 us -> 72.6 us  [the longest x1 70.2 us: on_device(): pl.pallas_call(functools.partial(kernel, n_z), out_shape=[*shapes, jax.Sh...]
where the time goes in v4:
time: 73.4 us; the launch traced here: 73.2 us
  Pallas kernels  72.6 us (99%)
    pallas_call x1, Pallas kernels, on_device(): pl.pallas_call(functools.partial(kernel, n_z), out_shape=[*shapes, jax.Sh...  70.2 us
    pallas_call x1, Pallas kernels, on_device(): pl.pallas_call(finish_kernel, out_shape=[*shapes, vector, vector], grid=(...  2.35 us

profile of v4, /device:TPU:1, one launch (start us, length us, event | category | flops | bytes accessed | tf_op | source)
XLA Modules:
  0.0 73.2 jit_solution(14620922119303686068)
XLA Ops:
  0.6 70.2 %scan_backward.1 = (bf16[128,4096]{1,0:T(8,128)(2,1)}, f32[128,128]{1,0:T(8,128)}, bf16[1024,128]{1,0:T(8,128)(2,1)}, bf16[1024,128]{1,0:T(8,128)(2,1)}, f32[8,128]{1,0:T(8,128)}) custom-call(f32[8]{0:T(128)} %dl_ref.1, f32[8]{0:T(128)} %sk_ref.1, bf16[128,128]{1,0:T(8,128)(2,1)} %raw_hbm.1, bf16[128,4096]{1,0:T(8,128)(2,1)} %x_hbm.1, ...), custom_call_target="tpu_custom_call" | custom-call | tf_op jit(solution)/shard_map/scan_backward/pallas_call | solution.py:632
  70.9 2.4 %finish.1 = (bf16[128,4096]{1,0:T(8,128)(2,1)}, f32[128,128]{1,0:T(8,128)}, bf16[1024,128]{1,0:T(8,128)(2,1)}, bf16[1024,128]{1,0:T(8,128)(2,1)}, f32[8]{0:T(128)}, /*index=5*/f32[8]{0:T(128)}) custom-call(bf16[128,4096]{1,0:T(8,128)(2,1)} %get-tuple-element.17.dx_in, f32[128,128]{1,0:T(8,128)} %get-tuple-element.18.draw_in, ...), custom_call_target="tpu_custom_call" | custom-call | tf_op jit(solution)/shard_map/finish/pallas_call | solution.py:658

commit v5 on v4

--- a/solution.py
+++ b/solution.py
@@ -66,6 +66,11 @@
         return carry
 
     lax.fori_loop(lo, hi, step, 0)
+
+
+def each(lo, hi, body):
+    for i in range(lo, hi):
+        body(i)
 
 
 def several(lo, hi, at_once, body):
@@ -147,9 +152,9 @@
         def _():
             greet(dev_y(j))
 
-    loop(1, n_t, lambda j: greet(dev_t(j)))
-    loop(1, n_y, greet_y)
-    loop(1, n_z, lambda j: greet(dev_z(j)))
+    each(1, n_t, lambda j: greet(dev_t(j)))
+    each(1, n_y, greet_y)
+    each(1, n_z, lambda j: greet(dev_z(j)))
     spot = lax.broadcasted_iota(jnp.int32, (1, Q), 1)
     params = jnp.zeros((1, Q), F32)
     for h in range(8):
@@ -166,7 +171,7 @@
     pl.semaphore_wait(barrier, n_t - 1 + n_y - n_y // y_lows + n_z - 1)
 
     def own_copy(j):
-        return remote(own_s, gath.at[me], own_sem, (j,), (j,), dev_t(lax.rem(j + 3, n_t - 1) + 1))
+        return remote(own_s, gath.at[me], own_sem, (j,), (j,), dev_t((j + 3) % (n_t - 1) + 1))
 
     def saved_copy(k):
         return remote(saved_s.at[k - 1], esaved.at[me], saved_sem, (k,), (me,), {"tensor": 2 * k})
@@ -183,7 +188,7 @@
         def _():
             esaved[me] = saved_s[k - 1]
 
-    loop(1, n_t, lambda j: own_copy(j).start())
+    each(1, n_t, lambda j: own_copy(j).start())
     loop(1, n_t // 2, send_saved)
     gath[me] = own_s[...]
 
@@ -202,7 +207,7 @@
 
     loop(0, GROUPS, turn)
 
-    loop(1, n_t, lambda j: own_copy(j).wait())
+    each(1, n_t, lambda j: own_copy(j).wait())
     params = gath[...].reshape(n_t, Q)
     for h in range(8):
         a_s[pl.ds(h, n_t, stride=8), :] = jnp.broadcast_to(params[:, h : h + 1], (n_t, Q))
@@ -520,10 +525,10 @@
         def copy(j):
             return remote(source, landing.at[at], sum_sem, (base + j,), (base + j,), dev(j))
 
-        loop(1, n, lambda j: copy(j).start())
+        each(1, n, lambda j: copy(j).start())
         landing[at] = source[...]
         beside()
-        loop(1, n, lambda j: copy(j).wait())
+        each(1, n, lambda j: copy(j).wait())
         return jnp.sum(landing[...], axis=0)
 
     stores = [

time: 73.4 us -> 73.4 us (level)
  no operation moved by 1% of the time
where the time goes in v5:
time: 73.4 us; the launch traced here: 73.2 us
  Pallas kernels  72.6 us (99%)
    pallas_call x1, Pallas kernels, on_device(): pl.pallas_call(functools.partial(kernel, n_z), out_shape=[*shapes, jax.Sh...  70.2 us
    pallas_call x1, Pallas kernels, on_device(): pl.pallas_call(finish_kernel, out_shape=[*shapes, vector, vector], grid=(...  2.35 us

profile of v5, /device:TPU:1, one launch (start us, length us, event | category | flops | bytes accessed | tf_op | source)
XLA Modules:
  0.0 73.2 jit_solution(5208076944977180329)
XLA Ops:
  0.6 70.2 %scan_backward.1 = (bf16[128,4096]{1,0:T(8,128)(2,1)}, f32[128,128]{1,0:T(8,128)}, bf16[1024,128]{1,0:T(8,128)(2,1)}, bf16[1024,128]{1,0:T(8,128)(2,1)}, f32[8,128]{1,0:T(8,128)}) custom-call(f32[8]{0:T(128)} %dl_ref.1, f32[8]{0:T(128)} %sk_ref.1, bf16[128,128]{1,0:T(8,128)(2,1)} %raw_hbm.1, bf16[128,4096]{1,0:T(8,128)(2,1)} %x_hbm.1, ...), custom_call_target="tpu_custom_call" | custom-call | tf_op jit(solution)/shard_map/scan_backward/pallas_call | solution.py:637
  70.9 2.4 %finish.1 = (bf16[128,4096]{1,0:T(8,128)(2,1)}, f32[128,128]{1,0:T(8,128)}, bf16[1024,128]{1,0:T(8,128)(2,1)}, bf16[1024,128]{1,0:T(8,128)(2,1)}, f32[8]{0:T(128)}, /*index=5*/f32[8]{0:T(128)}) custom-call(bf16[128,4096]{1,0:T(8,128)(2,1)} %get-tuple-element.17.dx_in, f32[128,128]{1,0:T(8,128)} %get-tuple-element.18.draw_in, ...), custom_call_target="tpu_custom_call" | custom-call | tf_op jit(solution)/shard_map/finish/pallas_call | solution.py:663
